TPU v7x, 512 devices: a whole 4x4x16 slice. The times are simulated.
512 devices in a mesh: layer: 16 (over z), col: 32 (over x, y, core).
Axes of the slice: x: 4, y: 4, z: 16, core: 2. Of those that a mesh axis runs over, the one named last changes fastest.
Arguments:
- iterate: float32 [16, 32, 4, 128, 128], P('layer', 'col'), as said below
- residual_in: float32 [16, 32, 4, 128, 128], P('layer', 'col'), as said below
- direction_in: float32 [16, 32, 4, 128, 128], P('layer', 'col'), as said below
- previous_rz: float32 [128], replicated, may hold values from 262144 to 1048576
- local_schur: float32 [16, 32, 512, 512], P('layer', 'col'), as said below
- local_inverse: float32 [16, 32, 512, 512], P('layer', 'col'), as said below
- coarse_inverse: float32 [1024, 1024], P(('layer', 'col')), as said below
- face_included: int32 [16, 32, 4], P('layer', 'col'), may hold values from 0 to 1, as said below
Outputs:
- iterate_out: float32 [16, 32, 4, 128, 128], P('layer', 'col')
- residual_out: float32 [16, 32, 4, 128, 128], P('layer', 'col')
- direction_out: float32 [16, 32, 4, 128, 128], P('layer', 'col')
- rz_out: float32 [128], replicated
Inputs may be any that keep to these rules, and one draw needn't show every extreme that they name: `face_included`: 1 where the face is part of the interface; the two subdomains that share a face carry the same flag for it; the lower faces of the first layer and the upper faces of the last layer are 0. `residual_in`: a face shared by two subdomains holds the same values on both. `direction_in`: a face shared by two subdomains holds the same values on both. `iterate`: a face shared by two subdomains holds the same values on both. `coarse_inverse`: symmetric positive definite. `local_schur`: each matrix symmetric positive definite. `local_inverse`: each matrix symmetric positive definite.
All inputs are finite; a program needn't handle non-finite values.
Results may differ from a plain program's by a relative error of at most 0.0002.
Values sent between devices are 32-bit elements; how exact they have to be, the bound alone decides.
A program may use at most 64 MiB of HBM per device.

v0:
```python
import jax
import jax.numpy as jnp
from jax import lax
from jax.sharding import PartitionSpec as P


def with_halo(cells, sides, width, closed):
    for axis, dim in sides:
        count = lax.axis_size(axis)
        ends = count if closed else count - 1
        head = lax.slice_in_dim(cells, 0, width, axis=dim)
        tail = lax.slice_in_dim(cells, cells.shape[dim] - width, cells.shape[dim], axis=dim)
        cells = jnp.concatenate(
            [
                lax.ppermute(tail, axis, [(i, (i + 1) % count) for i in range(ends)]),
                cells,
                lax.ppermute(head, axis, [((i + 1) % count, i) for i in range(ends)]),
            ],
            axis=dim,
        )
    return cells


def free_of_means(field):
    return field - jnp.mean(field, axis=1, keepdims=True)


def multiply(matrix, field):
    faces, face_size, columns = field.shape
    result = jnp.dot(
        matrix,
        field.reshape(faces * face_size, columns),
        precision=lax.Precision.HIGHEST,
        preferred_element_type=jnp.float32,
    )
    return result.reshape(faces, face_size, columns)


def assemble(contrib):
    layer_part = with_halo(contrib[0:2], (("layer", 0),), 1, False)
    column_part = with_halo(contrib[2:4], (("col", 0),), 1, True)
    return jnp.concatenate(
        [
            contrib[0:2] + jnp.stack([layer_part[0], layer_part[3]]),
            contrib[2:4] + jnp.stack([column_part[0], column_part[3]]),
        ],
        0,
    )


def per_device(
    iterate,
    residual_in,
    direction_in,
    previous_rz,
    local_schur,
    local_inverse,
    coarse_inverse,
    face_included,
):
    included = face_included[0, 0].astype(jnp.float32)[:, None, None]
    residual = included * residual_in[0, 0]
    previous = included * direction_in[0, 0]
    schur = local_schur[0, 0]
    inner = multiply(local_inverse[0, 0], free_of_means(0.5 * residual))
    dual = included * free_of_means(inner)
    coarse_res = jnp.stack([residual[1], residual[3]]).mean(axis=1)
    correction = jnp.dot(
        coarse_inverse,
        lax.all_gather(coarse_res, ("layer", "col"), axis=0, tiled=True),
        precision=lax.Precision.HIGHEST,
        preferred_element_type=jnp.float32,
    )
    owned = jnp.stack([included[1, 0], included[3, 0]])
    correction = correction * owned
    zero_face = jnp.zeros_like(correction[0])
    addon = jnp.stack([zero_face, correction[0], zero_face, correction[1]])[:, None, :]
    contrib = 0.5 * dual + addon
    precond = assemble(contrib)
    rz_out = lax.psum(0.5 * jnp.sum(residual * precond, axis=(0, 1)), ("layer", "col"))
    beta = rz_out / previous_rz
    direction = precond + beta * previous
    local_image = included * multiply(schur, direction)
    curvature = lax.psum(jnp.sum(direction * local_image, axis=(0, 1)), ("layer", "col"))
    alpha = rz_out / curvature
    image = assemble(local_image)
    iterate_out = iterate[0, 0] + alpha * direction
    residual_out = residual - alpha * image
    return (iterate_out[None, None], residual_out[None, None], direction[None, None], rz_out)


def solution(mesh):
    placed = (
        P("layer", "col", None, None, None),
        P("layer", "col", None, None, None),
        P("layer", "col", None, None, None),
        P(),
        P("layer", "col", None, None),
        P("layer", "col", None, None),
        P(("layer", "col"), None),
        P("layer", "col", None),
    )
    return jax.shard_map(
        per_device,
        mesh=mesh,
        in_specs=placed,
        out_specs=(
            P("layer", "col", None, None, None),
            P("layer", "col", None, None, None),
            P("layer", "col", None, None, None),
            P(),
        ),
        check_vma=False,
    )
```

profile of v0, /device:TPU:1, one launch (start us, length us, event | category | flops | bytes accessed | tf_op | source)
XLA Modules:
  0.0 364.4 jit_solution(13278303148485375286)
XLA Ops:
  0.6 0.0 copy-start
  0.6 0.7 fusion.13
  1.4 0.6 fusion.12
  2.0 1.1 multiply_reduce_fusion.2
  3.2 1.3 convolution_bitcast_fusion.1
  4.4 0.1 reshape.170
  4.5 0.1 copy.21
  4.7 0.2 reduce_sum.46
  4.9 0.1 copy.20
  5.0 123.3 %all-gather = f32[512,2,128]{2,1,0:T(2,128)S(1)} all-gather(f32[1,2,128]{2,1,0:T(2,128)S(1)} %multiply_bitcast_fusion), channel_id=1, replica_groups=mesh['layer'=16,'col'=32] {'layer','col'}, dimensions={0}, use_global_device_ids=true | all-gather | bytes 525312 | tf_op jit(solution)/shard_map/all_gather | solution.py:70
  128.3 1.4 maximum_reduce_fusion.1
  129.7 0.4 fusion
  130.1 0.1 multiply_add_fusion.1
  130.3 2.7 collective-permute-start
  133.0 2.4 collective-permute-start.3
  135.3 3.2 collective-permute-start.2
  138.6 1.4 collective-permute-start.1
  140.0 4.6 %collective-permute-done.1 = f32[1,128,128]{2,1,0:T(8,128)S(1)} collective-permute-done((f32[1,128,128]{2,1,0:T(8,128)S(1)}, f32[1,128,128]{2,1,0:T(8,128)S(1)}, u32[]{:S(2)}, u32[]{:S(2)}) %collective-permute-start.1) | collective-permute-done | bytes 65568 | tf_op jit(solution)/shard_map/ppermute | solution.py:17
  144.7 0.1 multiply_reduce_fusion.1
  144.8 103.8 %psum.14 = f32[128]{0:T(128)S(1)} all-reduce(f32[128]{0:T(128)S(1)} %broadcast_multiply_fusion.3), channel_id=1, replica_groups=mesh['layer'=16,'col'=32] {'layer','col'}, use_global_device_ids=true, to_apply=%region_4.0 | all-reduce | flops 128 | bytes 1024 | tf_op jit(solution)/shard_map/psum | solution.py:80
  248.6 0.1 fusion.5
  248.7 1.2 convolution_bitcast_fusion
  249.9 0.1 copy.23
  250.1 0.2 multiply_reduce_fusion
  250.3 1.3 collective-permute-start.4
  251.6 2.1 collective-permute-start.6
  253.7 1.3 collective-permute-start.5
  255.0 2.4 collective-permute-start.7
  257.4 105.0 %psum.15 = f32[128]{0:T(128)S(1)} all-reduce(f32[128]{0:T(128)S(1)} %get-tuple-element.6), channel_id=1, replica_groups=mesh['layer'=16,'col'=32] {'layer','col'}, use_global_device_ids=true, to_apply=%region_6.0 | all-reduce | flops 128 | bytes 1024 | tf_op jit(solution)/shard_map/psum | solution.py:84
  362.5 0.9 copy-done.1
  363.3 0.1 copy-done.4
  363.4 1.0 multiply_add_fusion
  (35 shorter events, 0.3 us)
Async XLA Ops:
  0.6 2.5 copy-start
  128.3 1.4 copy-start.5
  130.3 9.7 %collective-permute-start = (f32[1,128,128]{2,1,0:T(8,128)S(1)}, f32[1,128,128]{2,1,0:T(8,128)S(1)}, u32[]{:S(2)}, u32[]{:S(2)}) collective-permute-start(f32[1,128,128]{2,1,0:T(8,128)S(1)} %get-tuple-element.18), channel_id=1, source_target_pairs={{0,32},{32,64},{64,96},{96,128},{128,160},{160,192},{192,224},{224... | collective-permute-start | bytes 196616 | tf_op jit(solution)/shard_map/ppermute | solution.py:15
  133.0 7.0 %collective-permute-start.3 = (f32[1,128,128]{2,1,0:T(8,128)S(1)}, f32[1,128,128]{2,1,0:T(8,128)S(1)}, u32[]{:S(2)}, u32[]{:S(2)}) collective-permute-start(f32[1,128,128]{2,1,0:T(8,128)S(1)} %get-tuple-element.19), channel_id=1, source_target_pairs={{1,0},{2,1},{3,2},{4,3},{5,4},{6,5},{7,6},{8,7},{9,8},{10,9},{11,1... | collective-permute-start | bytes 196616 | tf_op jit(solution)/shard_map/ppermute | solution.py:17
  135.3 4.7 %collective-permute-start.2 = (f32[1,128,128]{2,1,0:T(8,128)S(1)}, f32[1,128,128]{2,1,0:T(8,128)S(1)}, u32[]{:S(2)}, u32[]{:S(2)}) collective-permute-start(f32[1,128,128]{2,1,0:T(8,128)S(1)} %get-tuple-element.20), channel_id=1, source_target_pairs={{0,1},{1,2},{2,3},{3,4},{4,5},{5,6},{6,7},{7,8},{8,9},{9,10},{10,1... | collective-permute-start | bytes 196616 | tf_op jit(solution)/shard_map/ppermute | solution.py:15
  138.6 110.1 %copy-start.3 = (f32[1,1,512,512]{3,2,1,0:T(8,128)S(1)}, f32[1,1,512,512]{3,2,1,0:T(8,128)}, u32[]{:S(2)}) copy-start(f32[1,1,512,512]{3,2,1,0:T(8,128)} %param.12) | copy-start | bytes 3145732
  138.6 6.0 %collective-permute-start.1 = (f32[1,128,128]{2,1,0:T(8,128)S(1)}, f32[1,128,128]{2,1,0:T(8,128)S(1)}, u32[]{:S(2)}, u32[]{:S(2)}) collective-permute-start(f32[1,128,128]{2,1,0:T(8,128)S(1)} %get-tuple-element.21), channel_id=1, source_target_pairs={{32,0},{64,32},{96,64},{128,96},{160,128},{192,160},{224,192},{256... | collective-permute-start | bytes 196616 | tf_op jit(solution)/shard_map/ppermute | solution.py:17
  144.6 103.9 %copy-start.2 = (f32[1,1,4,128,128]{4,3,2,1,0:T(8,128)S(1)}, f32[1,1,4,128,128]{4,3,2,1,0:T(8,128)}, u32[]{:S(2)}) copy-start(f32[1,1,4,128,128]{4,3,2,1,0:T(8,128)} %param.10) | copy-start | bytes 786436
  144.7 103.8 %copy-start.6 = (f32[128]{0:T(128)S(1)}, f32[128]{0:T(128)}, u32[]{:S(2)}) copy-start(f32[128]{0:T(128)} %param.11) | copy-start | bytes 1540
  248.6 113.8 %copy-start.7 = (f32[128]{0:T(128)}, f32[128]{0:T(128)S(1)}, u32[]{:S(2)}) copy-start(f32[128]{0:T(128)S(1)} %psum.14) | copy-start | bytes 1540
  250.3 112.1 %collective-permute-start.4 = (f32[1,128,128]{2,1,0:T(8,128)S(1)}, f32[1,128,128]{2,1,0:T(8,128)S(1)}, u32[]{:S(2)}, u32[]{:S(2)}) collective-permute-start(f32[1,128,128]{2,1,0:T(8,128)S(1)} %get-tuple-element.12), channel_id=1, source_target_pairs={{0,32},{32,64},{64,96},{96,128},{128,160},{160,192},{192,224},{224... | collective-permute-start | bytes 196616 | tf_op jit(solution)/shard_map/ppermute | solution.py:15
  251.6 110.8 %collective-permute-start.6 = (f32[1,128,128]{2,1,0:T(8,128)S(1)}, f32[1,128,128]{2,1,0:T(8,128)S(1)}, u32[]{:S(2)}, u32[]{:S(2)}) collective-permute-start(f32[1,128,128]{2,1,0:T(8,128)S(1)} %get-tuple-element.13), channel_id=1, source_target_pairs={{0,1},{1,2},{2,3},{3,4},{4,5},{5,6},{6,7},{7,8},{8,9},{9,10},{10,1... | collective-permute-start | bytes 196616 | tf_op jit(solution)/shard_map/ppermute | solution.py:15
  253.7 108.7 %collective-permute-start.5 = (f32[1,128,128]{2,1,0:T(8,128)S(1)}, f32[1,128,128]{2,1,0:T(8,128)S(1)}, u32[]{:S(2)}, u32[]{:S(2)}) collective-permute-start(f32[1,128,128]{2,1,0:T(8,128)S(1)} %get-tuple-element.14), channel_id=1, source_target_pairs={{32,0},{64,32},{96,64},{128,96},{160,128},{192,160},{224,192},{256... | collective-permute-start | bytes 196616 | tf_op jit(solution)/shard_map/ppermute | solution.py:17
  255.0 107.4 %collective-permute-start.7 = (f32[1,128,128]{2,1,0:T(8,128)S(1)}, f32[1,128,128]{2,1,0:T(8,128)S(1)}, u32[]{:S(2)}, u32[]{:S(2)}) collective-permute-start(f32[1,128,128]{2,1,0:T(8,128)S(1)} %get-tuple-element.15), channel_id=1, source_target_pairs={{1,0},{2,1},{3,2},{4,3},{5,4},{6,5},{7,6},{8,7},{9,8},{10,9},{11,1... | collective-permute-start | bytes 196616 | tf_op jit(solution)/shard_map/ppermute | solution.py:17
  362.4 1.0 copy-start.1
  362.4 1.0 copy-start.4
where the time goes:
time: 365 us; the launch traced here: 364 us
  blocking collectives  332 us (91%)
  starting transfers between devices  16.8 us (5%)
  other arithmetic  5.06 us (1%)
  waiting for transfers between devices  4.59 us (1%)
    all_gather x1, blocking collectives, per_device(): lax.all_gather(coarse_res, ('layer', 'col'), axis=0, tiled=True)  123 us
    psum x1, blocking collectives, per_device(): lax.psum(jnp.sum(direction * local_image, axis=(0, 1)), ('layer', 'col'))  105 us
    psum x1, blocking collectives, per_device(): lax.psum(0.5 * jnp.sum(residual * precond, axis=(0, 1)), ('layer', 'col'))  104 us
    ppermute x4, starting transfers between devices, with_halo(): lax.ppermute(tail, axis, [(i, (i + 1) % count) for i in range(ends)])  9.33 us
    ppermute x4, starting transfers between devices, with_halo(): lax.ppermute(head, axis, [((i + 1) % count, i) for i in range(ends)])  7.45 us
  transfers between devices with their start and end apart: 8, of which 1 were waited for; matrix products, arithmetic and copies ran while one was open for 0% of the time, Pallas kernels for 0%

commit v1 on v0

v1 whole, which is shorter than its diff:
```python
import functools
import jax
import jax.numpy as jnp
from jax import lax
from jax.experimental import pallas as pl
from jax.experimental.pallas import tpu as pltpu
from jax.sharding import PartitionSpec as P

MESH = pl.DeviceIdType.MESH
HIGH = lax.Precision.HIGHEST


def mm(a, b):
    return jnp.dot(a, b, precision=HIGH, preferred_element_type=jnp.float32)


def wait_all(ref, count, sem):
    part = ref.at[pl.ds(0, count)]
    pltpu.make_async_copy(part, part, sem).wait()


def kernel(
    layers,
    cols,
    inc_ref,
    prz_ref,
    x_hbm,
    r_hbm,
    q_hbm,
    s_hbm,
    m_hbm,
    c_hbm,
    xo_hbm,
    ro_hbm,
    do_hbm,
    rz_ref,
    xv,
    rv,
    qv,
    sv,
    mv,
    cv,
    outv,
    rhs,
    sqe,
    spv,
    pd,
    hsrc,
    hdst,
    rsend,
    rbuf,
    rflat,
    cbuf_a,
    cbuf_b,
    cfull,
    psend,
    ybuf,
    cpad,
    a1send,
    a1buf,
    a2send,
    a2buf,
    in_sem,
    out_sem,
    send_sem,
    recv_sem,
    hsend_sem,
    hrecv_sem,
):
    fb = xv.shape[0] // 4
    width = 2 * cols
    lanes = rflat.shape[0]
    per = lanes // width
    lay = lax.axis_index("layer")
    col = lax.axis_index("col")
    below = lax.rem(lay + layers - 1, layers)
    above = lax.rem(lay + 1, layers)
    left = lax.rem(col + cols - 1, cols)
    right = lax.rem(col + 1, cols)

    def load(src, dst, i):
        return pltpu.make_async_copy(src, dst, in_sem.at[i])

    loads = [
        load(r_hbm, rv, 0),
        load(c_hbm, cv, 1),
        load(m_hbm, mv, 2),
        load(q_hbm, qv, 3),
        load(s_hbm, sv, 4),
        load(x_hbm, xv, 5),
    ]
    for one in loads:
        one.start()

    barrier = pltpu.get_barrier_semaphore()

    def greet(l, c):
        pl.semaphore_signal(barrier, inc=1, device_id=(l, c), device_id_type=MESH)

    def others(n, me, act):
        def body(k, carry):
            act(lax.rem(me + k, n))
            return carry

        lax.fori_loop(1, n, body, 0)

    def greet_layer(l):
        greet(l, col)
        greet(l, left)

    others(layers, lay, greet_layer)
    others(cols, col, lambda c: greet(lay, c))

    def send(src, dst, i, l, c):
        pltpu.make_async_remote_copy(
            src_ref=src,
            dst_ref=dst,
            send_sem=send_sem.at[i],
            recv_sem=recv_sem.at[i],
            device_id=(l, c),
            device_id_type=MESH,
        ).start()

    def face(f):
        return pl.ds(f * fb, fb)

    def halo(i):
        for f, g, l, c in ((0, 1, below, col), (1, 0, above, col), (2, 3, lay, left), (3, 2, lay, right)):
            pltpu.make_async_remote_copy(
                src_ref=hsrc.at[i, f],
                dst_ref=hdst.at[i, g],
                send_sem=hsend_sem.at[i],
                recv_sem=hrecv_sem.at[i],
                device_id=(l, c),
                device_id_type=MESH,
            ).start()

    def assembled(i, own, f):
        got = hdst[i, f]
        if f == 0:
            got = jnp.where(lay > 0, got, 0.0)
        if f == 1:
            got = jnp.where(lay < layers - 1, got, 0.0)
        return own + got

    inc = [inc_ref[f].astype(jnp.float32) for f in range(4)]

    loads[0].wait()
    means = []
    for f in range(4):
        res = inc[f] * rv[face(f), :]
        rv[face(f), :] = res
        means.append(jnp.mean(res, axis=0, keepdims=True))
    rsend[0:1, :] = means[1]
    rsend[1:2, :] = means[3]
    loads[1].wait()

    pl.semaphore_wait(barrier, 2 * (layers - 1) + cols - 1)

    others(cols, col, lambda c: send(rsend, rbuf.at[col], 0, lay, c))

    def block(l):
        return cv.at[:, pl.ds(pl.multiple_of((l // per) * lanes, lanes), lanes)]

    def send_rows(l):
        send(block(l), cbuf_a.at[lay], 1, l, col)
        send(block(l), cbuf_b.at[lay], 2, l, right)

    others(layers, lay, send_rows)
    send(block(lay), cbuf_b.at[lay], 2, lay, right)
    rbuf[pl.ds(col, 1)] = rsend[...][None]
    cbuf_a[pl.ds(lay, 1)] = cv[:, pl.ds(pl.multiple_of((lay // per) * lanes, lanes), lanes)][None]

    for f in range(4):
        spv[face(f), :] = 0.5 * (rv[face(f), :] - means[f])
    loads[2].wait()
    inner = mm(mv[...], spv[...])
    rz = jnp.zeros_like(means[0])
    for f in range(4):
        part = inner[f * fb : (f + 1) * fb]
        half = 0.5 * (inc[f] * (part - jnp.mean(part, axis=0, keepdims=True)))
        hsrc[0, f] = half
        rz += jnp.sum(rv[face(f), :] * half, axis=0, keepdims=True)
    halo(0)

    loads[3].wait()
    row = lax.broadcasted_iota(jnp.int32, (fb, 128), 1)
    for f in range(4):
        prev = inc[f] * qv[face(f), :]
        qv[face(f), :] = prev
        rhs[face(f), 0:128] = prev
        rhs[face(f), 128:256] = jnp.where(row == f, 1.0, 0.0)
    loads[4].wait()
    sqe[...] = mm(sv[...], rhs[...])
    qq = jnp.zeros_like(rz)
    hq = []
    ke = []
    for f in range(4):
        sq = inc[f] * sqe[face(f), 0:128]
        se = inc[f] * sqe[face(f), 128:256]
        sqe[face(f), 128:256] = se
        hsrc[1, f] = sq
        qq += jnp.sum(qv[face(f), :] * sq, axis=0, keepdims=True)
        hq.append(jnp.sum(sq, axis=0, keepdims=True))
        ke.append(jnp.sum(se, axis=0, keepdims=True))
    halo(1)

    wait_all(cbuf_a, layers - 1, recv_sem.at[1])
    wait_all(cbuf_b, layers, recv_sem.at[2])
    for l in range(layers):
        one = cbuf_a[l]
        two = cbuf_b[l]
        up = (l + 1) % layers
        cfull[4 * up : 4 * up + 1, :] = one[0:1]
        cfull[4 * l + 1 : 4 * l + 2, :] = one[0:1]
        cfull[4 * l + 2 : 4 * l + 3, :] = two[1:2]
        cfull[4 * l + 3 : 4 * l + 4, :] = one[1:2]
    lane = lax.broadcasted_iota(jnp.int32, cfull.shape, 1)
    mine = (lane // width) == lax.rem(lay, per)
    coarse = jnp.where(mine, cfull[...], 0.0)
    wait_all(rbuf, cols - 1, recv_sem.at[0])
    for c in range(cols):
        pair = rbuf[c]
        for k in range(per):
            rflat[k * width + 2 * c : k * width + 2 * c + 2, :] = pair
    part = mm(coarse, rflat[...])
    for l in range(layers):
        psend[l] = part[4 * l : 4 * l + 4]
    others(layers, lay, lambda l: send(psend.at[l], ybuf.at[lay], 3, l, col))
    ybuf[pl.ds(lay, 1)] = psend[pl.ds(lay, 1)]

    wait_all(hdst.at[0], 4, hrecv_sem.at[0])
    for f in range(4):
        pd[face(f), :] = assembled(0, hsrc[0, f], f)
    spv[...] = mm(sv[...], pd[...])
    pp = jnp.zeros_like(rz)
    pq = jnp.zeros_like(rz)
    gp = []
    for f in range(4):
        sp = inc[f] * spv[face(f), :]
        spv[face(f), :] = sp
        here = pd[face(f), :]
        pp += jnp.sum(here * sp, axis=0, keepdims=True)
        pq += jnp.sum(here * hsrc[1, f], axis=0, keepdims=True)
        gp.append(jnp.sum(sp, axis=0, keepdims=True))
    cpad[...] = jnp.zeros_like(cpad)

    wait_all(ybuf, layers - 1, recv_sem.at[3])
    total = jnp.sum(ybuf[...], axis=0)
    cor = [inc[f] * total[f : f + 1] for f in range(4)]
    for f in range(4):
        cpad[f : f + 1, :] = cor[f]
    rz += float(fb) * (means[1] * cor[1] + means[3] * cor[3])
    for f in range(4):
        kc = gp[f] * 2.0
        for g in range(4):
            kc += ke[f][:, g : g + 1] * cor[g]
        pp += cor[f] * kc
        pq += cor[f] * hq[f]
    a1send[0:1, :] = rz
    a1send[1:2, :] = pp
    a1send[2:3, :] = 2.0 * pq
    a1send[3:4, :] = qq
    others(layers, lay, lambda l: send(a1send, a1buf.at[lay], 4, l, col))
    a1buf[pl.ds(lay, 1)] = a1send[...][None]

    change = mm(sqe[:, 128:256], cpad[...])
    for f in range(4):
        hsrc[2, f] = spv[face(f), :] + change[f * fb : (f + 1) * fb]
        pd[face(f), :] = pd[face(f), :] + cor[f]
    halo(2)

    wait_all(a1buf, layers - 1, recv_sem.at[4])
    a2send[...] = jnp.sum(a1buf[...], axis=0)
    others(cols, col, lambda c: send(a2send, a2buf.at[col], 5, lay, c))
    a2buf[pl.ds(col, 1)] = a2send[...][None]
    wait_all(hdst.at[1], 4, hrecv_sem.at[1])
    for f in range(4):
        sqe[face(f), 0:128] = assembled(1, hsrc[1, f], f)
    wait_all(hdst.at[2], 4, hrecv_sem.at[2])
    for f in range(4):
        spv[face(f), :] = assembled(2, hsrc[2, f], f)
    loads[5].wait()

    wait_all(a2buf, cols - 1, recv_sem.at[5])
    sums = jnp.sum(a2buf[...], axis=0)
    rz_all = sums[0:1]
    beta = rz_all / prz_ref[...]
    curvature = sums[1:2] + beta * (sums[2:3] + beta * sums[3:4])
    alpha = rz_all / curvature
    rz_ref[...] = rz_all
    outs = []
    for f in range(4):
        direction = pd[face(f), :] + beta * qv[face(f), :]
        outv[0, f] = direction
        outv[1, f] = xv[face(f), :] + alpha * direction
        image = spv[face(f), :] + beta * sqe[face(f), 0:128]
        outv[2, f] = rv[face(f), :] - alpha * image
    for i, dst in enumerate((do_hbm, xo_hbm, ro_hbm)):
        one = pltpu.make_async_copy(outv.at[i], dst, out_sem.at[i])
        one.start()
        outs.append(one)

    wait_all(rbuf, cols - 1, send_sem.at[0])
    wait_all(cbuf_a, layers - 1, send_sem.at[1])
    wait_all(cbuf_b, layers, send_sem.at[2])
    wait_all(ybuf, layers - 1, send_sem.at[3])
    wait_all(a1buf, layers - 1, send_sem.at[4])
    wait_all(a2buf, cols - 1, send_sem.at[5])
    for i in range(3):
        wait_all(hsrc.at[i], 4, hsend_sem.at[i])
    for one in outs:
        one.wait()


def solution(mesh):
    layers, cols = mesh.shape["layer"], mesh.shape["col"]

    def per_device(
        iterate,
        residual_in,
        direction_in,
        previous_rz,
        local_schur,
        local_inverse,
        coarse_inverse,
        face_included,
    ):
        _, _, _, fb, rhs = iterate.shape
        nb = 4 * fb
        nco = coarse_inverse.shape[1]
        lanes = min(128, nco)
        f32 = jnp.float32
        flat = [v.reshape(nb, rhs) for v in (iterate, residual_in, direction_in)]
        hbm = pl.BlockSpec(memory_space=pltpu.HBM)
        vmem = pl.BlockSpec(memory_space=pltpu.VMEM)
        field = jax.ShapeDtypeStruct((4, fb, rhs), f32)
        vec = pltpu.VMEM((nb, rhs), f32)
        mat = pltpu.VMEM((nb, nb), f32)
        xo, ro, do, rz = pl.pallas_call(
            functools.partial(kernel, layers, cols),
            out_shape=(field, field, field, jax.ShapeDtypeStruct((1, rhs), f32)),
            in_specs=[pl.BlockSpec(memory_space=pltpu.SMEM), vmem] + [hbm] * 6,
            out_specs=(hbm, hbm, hbm, vmem),
            scratch_shapes=[
                vec,
                vec,
                vec,
                mat,
                mat,
                pltpu.VMEM((2, nco), f32),
                pltpu.VMEM((3, 4, fb, rhs), f32),
                pltpu.VMEM((nb, 256), f32),
                pltpu.VMEM((nb, 256), f32),
                vec,
                vec,
                pltpu.VMEM((3, 4, fb, rhs), f32),
                pltpu.VMEM((3, 4, fb, rhs), f32),
                pltpu.VMEM((2, rhs), f32),
                pltpu.VMEM((cols, 2, rhs), f32),
                pltpu.VMEM((lanes, rhs), f32),
                pltpu.VMEM((layers, 2, lanes), f32),
                pltpu.VMEM((layers, 2, lanes), f32),
                pltpu.VMEM((4 * layers, lanes), f32),
                pltpu.VMEM((layers, 4, rhs), f32),
                pltpu.VMEM((layers, 4, rhs), f32),
                pltpu.VMEM((128, rhs), f32),
                pltpu.VMEM((4, rhs), f32),
                pltpu.VMEM((layers, 4, rhs), f32),
                pltpu.VMEM((4, rhs), f32),
                pltpu.VMEM((cols, 4, rhs), f32),
                pltpu.SemaphoreType.DMA((6,)),
                pltpu.SemaphoreType.DMA((3,)),
                pltpu.SemaphoreType.DMA((6,)),
                pltpu.SemaphoreType.DMA((6,)),
                pltpu.SemaphoreType.DMA((3,)),
                pltpu.SemaphoreType.DMA((3,)),
            ],
            compiler_params=pltpu.CompilerParams(
                collective_id=0, has_side_effects=True, vmem_limit_bytes=32 * 1024 * 1024
            ),
        )(
            face_included.reshape(4),
            previous_rz.reshape(1, rhs),
            *flat,
            local_schur.reshape(nb, nb),
            local_inverse.reshape(nb, nb),
            coarse_inverse,
        )
        shape = iterate.shape
        return xo.reshape(shape), ro.reshape(shape), do.reshape(shape), rz.reshape(rhs)

    placed = (
        P("layer", "col", None, None, None),
        P("layer", "col", None, None, None),
        P("layer", "col", None, None, None),
        P(),
        P("layer", "col", None, None),
        P("layer", "col", None, None),
        P(("layer", "col"), None),
        P("layer", "col", None),
    )
    return jax.shard_map(
        per_device,
        mesh=mesh,
        in_specs=placed,
        out_specs=(
            P("layer", "col", None, None, None),
            P("layer", "col", None, None, None),
            P("layer", "col", None, None, None),
            P(),
        ),
        check_vma=False,
    )
```

time: 365 us -> 55 us (0.15)
  blocking collectives: 332 us -> 0 us
  Pallas kernels: 0 us -> 45.4 us
  starting transfers between devices: 16.8 us -> 0 us
  local copies, waits for them, and re-layouts: 2.02 us -> 8.6 us
  other arithmetic: 5.06 us -> 0 us
  waiting for transfers between devices: 4.59 us -> 0 us
    psum x2 -> x0, blocking collectives: 209 us -> none  [the longest x1 105 us: per_device(): lax.psum(jnp.sum(direction * local_image, axis=(0, 1)), ('layer', 'col'))]
    all_gather x1 -> x0, blocking collectives: 123 us -> none  [per_device(): lax.all_gather(coarse_res, ('layer', 'col'), axis=0, tiled=True)]
    pallas_call x0 -> x1, Pallas kernels: none -> 45.4 us  [per_device(): pl.pallas_call(functools.partial(kernel, layers, cols), out_shape=(field,...]
    ppermute x8 -> x0, starting transfers between devices: 16.8 us -> none  [the longest x4 9.33 us: with_halo(): lax.ppermute(tail, axis, [(i, (i + 1) % count) for i in range(ends)])]
    unnamed x16 -> x20, local copies, waits for them, and re-layouts: 0.97 us -> 8.6 us
    ppermute x8 -> x0, waiting for transfers between devices: 4.59 us -> none  [the longest x4 4.58 us: with_halo(): lax.ppermute(head, axis, [((i + 1) % count, i) for i in range(ends)])]
  transfers between devices with their start and end apart: 8 -> 0, of which waited for: 1 -> 0; matrix products, arithmetic and copies ran while one was open for 0% -> 0% of each run, Pallas kernels for 0% -> 0%
where the time goes in v1:
time: 55 us; the launch traced here: 54.6 us
  Pallas kernels  45.4 us (83%)
  local copies, waits for them, and re-layouts  8.6 us (16%)
  between operations  0.67 us (1%)
    pallas_call x1, Pallas kernels, per_device(): pl.pallas_call(functools.partial(kernel, layers, cols), out_shape=(field,...  45.4 us
    unnamed x20, local copies, waits for them, and re-layouts  8.6 us

profile of v1, /device:TPU:1, one launch (start us, length us, event | category | flops | bytes accessed | tf_op | source)
XLA Modules:
  0.0 54.6 jit_solution(2917714492311055669)
XLA Ops:
  0.6 0.0 copy-start.5
  0.6 0.0 copy-start.6
  0.7 0.0 copy-start.7
  0.7 0.7 %copy-done.5 = f32[2,1024]{1,0:T(2,128)S(1)} copy-done((f32[2,1024]{1,0:T(2,128)S(1)}, f32[2,1024]{1,0:T(2,128)}, u32[]{:S(2)}) %copy-start.5) | copy-done | bytes 8216
  1.3 0.0 copy-done.6
  1.3 0.0 copy-done.7
  1.3 0.0 copy-start
  1.3 1.2 %copy-done = f32[1,1,512,512]{3,2,1,0:T(8,128)S(1)} copy-done((f32[1,1,512,512]{3,2,1,0:T(8,128)S(1)}, f32[1,1,512,512]{3,2,1,0:T(8,128)}, u32[]{:S(2)}) %copy-start) | copy-done | bytes 1048600
  2.6 0.0 copy-start.1
  2.6 1.2 %copy-done.1 = f32[1,1,512,512]{3,2,1,0:T(8,128)S(1)} copy-done((f32[1,1,512,512]{3,2,1,0:T(8,128)S(1)}, f32[1,1,512,512]{3,2,1,0:T(8,128)}, u32[]{:S(2)}) %copy-start.1) | copy-done | bytes 1048600
  3.8 0.0 copy-start.2
  3.8 0.9 %copy-done.2 = f32[1,1,4,128,128]{4,3,2,1,0:T(8,128)S(1)} copy-done((f32[1,1,4,128,128]{4,3,2,1,0:T(8,128)S(1)}, f32[1,1,4,128,128]{4,3,2,1,0:T(8,128)}, u32[]{:S(2)}) %copy-start.2) | copy-done | bytes 262168
  4.7 0.0 copy-start.3
  4.7 0.9 %copy-done.3 = f32[1,1,4,128,128]{4,3,2,1,0:T(8,128)S(1)} copy-done((f32[1,1,4,128,128]{4,3,2,1,0:T(8,128)S(1)}, f32[1,1,4,128,128]{4,3,2,1,0:T(8,128)}, u32[]{:S(2)}) %copy-start.3) | copy-done | bytes 262168
  5.7 0.0 copy-start.4
  5.7 0.9 %copy-done.4 = f32[1,1,4,128,128]{4,3,2,1,0:T(8,128)S(1)} copy-done((f32[1,1,4,128,128]{4,3,2,1,0:T(8,128)S(1)}, f32[1,1,4,128,128]{4,3,2,1,0:T(8,128)}, u32[]{:S(2)}) %copy-start.4) | copy-done | bytes 262168
  6.6 45.4 %shard_map.111 = (f32[4,128,128]{2,1,0:T(8,128)S(1)}, f32[4,128,128]{2,1,0:T(8,128)S(1)}, f32[4,128,128]{2,1,0:T(8,128)S(1)}, f32[1,128]{1,0:T(1,128)S(1)}) custom-call(s32[4]{0:T(128)S(1)} %bitcast.19, f32[1,128]{1,0:T(1,128)S(1)} %bitcast.20, f32[512,128]{1,0:T(8,128)S(1)} %bitcast.16, f32[512,128]{1,0:T(8,128)S(1)} %bitcast.17, f32[512,128]{1,0:T(8,128)S(1)} %bitcast.18, ...), custom_call_target="tpu_custom_call" | custom-call | tf_op jit(solution)/shard_map/pallas_call | solution.py:340
  52.0 0.7 %copy.16 = f32[1,1,4,128,128]{4,3,2,1,0:T(8,128)} copy(f32[1,1,4,128,128]{4,3,2,1,0:T(8,128)S(1)} %bitcast.15) | data formatting | bytes 524288
  52.7 0.7 %copy.17 = f32[1,1,4,128,128]{4,3,2,1,0:T(8,128)} copy(f32[1,1,4,128,128]{4,3,2,1,0:T(8,128)S(1)} %bitcast.14) | data formatting | bytes 524288
  53.4 0.7 %copy.18 = f32[1,1,4,128,128]{4,3,2,1,0:T(8,128)} copy(f32[1,1,4,128,128]{4,3,2,1,0:T(8,128)S(1)} %bitcast.13) | data formatting | bytes 524288
  54.1 0.5 copy.19
Async XLA Ops:
  0.6 0.7 %copy-start.5 = (f32[2,1024]{1,0:T(2,128)S(1)}, f32[2,1024]{1,0:T(2,128)}, u32[]{:S(2)}) copy-start(f32[2,1024]{1,0:T(2,128)} %c_hbm.1) | copy-start | bytes 24580
  0.6 0.7 %copy-start.6 = (s32[1,1,4]{2,1,0:T(1,128)S(1)}, s32[1,1,4]{2,1,0:T(1,128)}, u32[]{:S(2)}) copy-start(s32[1,1,4]{2,1,0:T(1,128)} %param.15) | copy-start | bytes 52
  0.7 0.7 %copy-start.7 = (f32[128]{0:T(128)S(1)}, f32[128]{0:T(128)}, u32[]{:S(2)}) copy-start(f32[128]{0:T(128)} %param.11) | copy-start | bytes 1540
  1.3 1.2 %copy-start = (f32[1,1,512,512]{3,2,1,0:T(8,128)S(1)}, f32[1,1,512,512]{3,2,1,0:T(8,128)}, u32[]{:S(2)}) copy-start(f32[1,1,512,512]{3,2,1,0:T(8,128)} %param.12) | copy-start | bytes 3145732
  2.6 1.2 %copy-start.1 = (f32[1,1,512,512]{3,2,1,0:T(8,128)S(1)}, f32[1,1,512,512]{3,2,1,0:T(8,128)}, u32[]{:S(2)}) copy-start(f32[1,1,512,512]{3,2,1,0:T(8,128)} %param.13) | copy-start | bytes 3145732
  3.8 0.9 %copy-start.2 = (f32[1,1,4,128,128]{4,3,2,1,0:T(8,128)S(1)}, f32[1,1,4,128,128]{4,3,2,1,0:T(8,128)}, u32[]{:S(2)}) copy-start(f32[1,1,4,128,128]{4,3,2,1,0:T(8,128)} %param.8) | copy-start | bytes 786436
  4.7 0.9 %copy-start.3 = (f32[1,1,4,128,128]{4,3,2,1,0:T(8,128)S(1)}, f32[1,1,4,128,128]{4,3,2,1,0:T(8,128)}, u32[]{:S(2)}) copy-start(f32[1,1,4,128,128]{4,3,2,1,0:T(8,128)} %param.9) | copy-start | bytes 786436
  5.7 0.9 %copy-start.4 = (f32[1,1,4,128,128]{4,3,2,1,0:T(8,128)S(1)}, f32[1,1,4,128,128]{4,3,2,1,0:T(8,128)}, u32[]{:S(2)}) copy-start(f32[1,1,4,128,128]{4,3,2,1,0:T(8,128)} %param.10) | copy-start | bytes 786436

commit v2 on v1

v2 whole, which is shorter than its diff:
```python
import functools
import jax
import jax.numpy as jnp
from jax import lax
from jax.experimental import pallas as pl
from jax.experimental.pallas import tpu as pltpu
from jax.sharding import PartitionSpec as P

MESH = pl.DeviceIdType.MESH
HIGH = lax.Precision.HIGHEST
VMEM_LIMIT = 60 * 1024 * 1024


def mm(a, b):
    return jnp.dot(a, b, precision=HIGH, preferred_element_type=jnp.float32)


def wait_all(ref, count, sem):
    part = ref.at[pl.ds(0, count)]
    pltpu.make_async_copy(part, part, sem).wait()


def kernel(
    layers,
    cols,
    inc_ref,
    prz_ref,
    x_hbm,
    r_hbm,
    q_hbm,
    s_hbm,
    m_hbm,
    c_hbm,
    out_ref,
    rz_ref,
    xv,
    rv,
    qv,
    sv,
    mv,
    cv,
    zc,
    csend,
    cbuf_a,
    cbuf_b,
    cfull,
    rhs,
    sqe,
    spv,
    pd,
    hsrc,
    hdst,
    rsend,
    rbuf,
    rflat,
    psend,
    ybuf,
    cpad,
    a1send,
    a1buf,
    a2send,
    a2buf,
    in_sem,
    send_sem,
    recv_sem,
    hsend_sem,
    hrecv_sem,
):
    fb = xv.shape[0] // 4
    width = 2 * cols
    nco = cv.shape[1]
    lanes = min(128, nco)
    npar = lanes // width
    nk = nco // lanes
    lay = lax.axis_index("layer")
    col = lax.axis_index("col")
    below = lax.rem(lay + layers - 1, layers)
    above = lax.rem(lay + 1, layers)
    left = lax.rem(col + cols - 1, cols)
    right = lax.rem(col + 1, cols)

    def load(src, dst, i):
        return pltpu.make_async_copy(src, dst, in_sem.at[i])

    loads = [
        load(r_hbm, rv, 0),
        load(c_hbm, cv, 1),
        load(m_hbm, mv, 2),
        load(q_hbm, qv, 3),
        load(s_hbm, sv, 4),
        load(x_hbm, xv, 5),
    ]
    loads[0].start()

    barrier = pltpu.get_barrier_semaphore()

    def greet(l, c):
        pl.semaphore_signal(barrier, inc=1, device_id=(l, c), device_id_type=MESH)

    def others(n, me, act):
        def body(k, carry):
            act(lax.rem(me + k, n))
            return carry

        lax.fori_loop(1, n, body, 0)

    def greet_col(c):
        greet(lay, c)
        greet(below, c)

    others(layers, lay, lambda l: greet(l, col))
    others(cols, col, greet_col)
    for one in loads[1:]:
        one.start()

    def send(src, dst, i, l, c):
        pltpu.make_async_remote_copy(
            src_ref=src,
            dst_ref=dst,
            send_sem=send_sem.at[i],
            recv_sem=recv_sem.at[i],
            device_id=(l, c),
            device_id_type=MESH,
        ).start()

    def face(f):
        return pl.ds(f * fb, fb)

    def halo(i, axis):
        pairs = ((0, 1, below, col), (1, 0, above, col), (2, 3, lay, left), (3, 2, lay, right))
        for f, g, l, c in pairs[2 * axis : 2 * axis + 2]:
            pltpu.make_async_remote_copy(
                src_ref=hsrc.at[i, f],
                dst_ref=hdst.at[i, g],
                send_sem=hsend_sem.at[i],
                recv_sem=hrecv_sem.at[i],
                device_id=(l, c),
                device_id_type=MESH,
            ).start()

    def assembled(i, own, f):
        got = hdst[i, f]
        if f == 0:
            got = jnp.where(lay > 0, got, 0.0)
        if f == 1:
            got = jnp.where(lay < layers - 1, got, 0.0)
        return own + got

    inc = [inc_ref[f].astype(jnp.float32) for f in range(4)]
    zc[...] = jnp.zeros_like(zc)
    rflat[...] = jnp.zeros_like(rflat)
    cpad[...] = jnp.zeros_like(cpad)

    loads[0].wait()
    means = []
    for f in range(4):
        res = inc[f] * rv[face(f), :]
        rv[face(f), :] = res
        mean = jnp.mean(res, axis=0, keepdims=True)
        means.append(mean)
        spv[face(f), :] = 0.5 * (res - mean)
    rsend[0:1, :] = means[1]
    rsend[1:2, :] = means[3]

    loads[1].wait()
    for k in range(nk):
        for row in range(2):
            zc[row, k : k + 1, :] = cv[row : row + 1, k * lanes : (k + 1) * lanes]
    turned = []
    for row in range(2):
        flip = zc[row].T
        whole = flip[0:width]
        for p in range(1, npar):
            whole += pltpu.roll(flip[p * width : (p + 1) * width], p * (128 // npar), 1)
        turned.append(whole)
    for c in range(cols):
        for row in range(2):
            csend[c, 2 * row : 2 * row + 2, :] = turned[row][2 * c : 2 * c + 2]

    loads[2].wait()
    inner = mm(mv[...], spv[...])
    rz = jnp.zeros_like(means[0])
    for f in range(4):
        part = inner[f * fb : (f + 1) * fb]
        half = 0.5 * (inc[f] * (part - jnp.mean(part, axis=0, keepdims=True)))
        hsrc[0, f] = half
        rz += jnp.sum(rv[face(f), :] * half, axis=0, keepdims=True)

    loads[3].wait()
    lane = lax.broadcasted_iota(jnp.int32, (fb, 128), 1)
    for f in range(4):
        prev = inc[f] * qv[face(f), :]
        qv[face(f), :] = prev
        rhs[face(f), 0:128] = prev
        rhs[face(f), 128:256] = jnp.where(lane == f, 1.0, 0.0)
    loads[4].wait()
    sqe[...] = mm(sv[...], rhs[...])
    qq = jnp.zeros_like(rz)
    hq = []
    ke = []
    for f in range(4):
        sq = inc[f] * sqe[face(f), 0:128]
        se = inc[f] * sqe[face(f), 128:256]
        sqe[face(f), 128:256] = se
        hsrc[1, f] = sq
        qq += jnp.sum(qv[face(f), :] * sq, axis=0, keepdims=True)
        hq.append(jnp.sum(sq, axis=0, keepdims=True))
        ke.append(jnp.sum(se, axis=0, keepdims=True))

    pl.semaphore_wait(barrier, layers - 1 + 2 * (cols - 1))

    others(layers, lay, lambda l: send(rsend, rbuf.at[lay], 0, l, col))

    def send_rows(c):
        send(csend.at[c], cbuf_a.at[col], 1, lay, c)
        send(csend.at[c], cbuf_b.at[col], 2, above, c)

    others(cols, col, send_rows)
    send(csend.at[col], cbuf_b.at[col], 2, above, col)
    halo(0, 0)
    halo(0, 1)
    halo(1, 1)
    rbuf[pl.ds(lay, 1)] = rsend[...][None]
    cbuf_a[pl.ds(col, 1)] = csend[pl.ds(col, 1)]

    wait_all(hdst.at[0], 4, hrecv_sem.at[0])
    for f in range(4):
        pd[face(f), :] = assembled(0, hsrc[0, f], f)
    spv[...] = mm(sv[...], pd[...])
    pp = jnp.zeros_like(rz)
    pq = jnp.zeros_like(rz)
    gp = []
    for f in range(4):
        sp = inc[f] * spv[face(f), :]
        spv[face(f), :] = sp
        here = pd[face(f), :]
        pp += jnp.sum(here * sp, axis=0, keepdims=True)
        pq += jnp.sum(here * hsrc[1, f], axis=0, keepdims=True)
        gp.append(jnp.sum(sp, axis=0, keepdims=True))

    wait_all(cbuf_a, cols - 1, recv_sem.at[1])
    wait_all(cbuf_b, cols, recv_sem.at[2])
    for c in range(cols):
        one = cbuf_a[c]
        two = cbuf_b[c]
        near = (c + 1) % cols
        for g in range(2):
            cfull[g, 4 * c : 4 * c + 1, :] = two[g : g + 1]
            cfull[g, 4 * c + 1 : 4 * c + 2, :] = one[g : g + 1]
            cfull[g, 4 * near + 2 : 4 * near + 3, :] = one[2 + g : 3 + g]
            cfull[g, 4 * c + 3 : 4 * c + 4, :] = one[2 + g : 3 + g]
    coarse = cfull[0] + pltpu.roll(cfull[1], nk, 1)
    wait_all(rbuf, layers - 1, recv_sem.at[0])
    for l in range(layers):
        at = (l % npar) * (128 // npar) + l // npar
        for g in range(2):
            rflat[at + g * nk : at + g * nk + 1, :] = rbuf[l, g : g + 1, :]
    part = mm(coarse, rflat[...])
    for c in range(cols):
        psend[c] = part[4 * c : 4 * c + 4]
    others(cols, col, lambda c: send(psend.at[c], ybuf.at[col], 3, lay, c))
    halo(1, 0)
    ybuf[pl.ds(col, 1)] = psend[pl.ds(col, 1)]

    wait_all(ybuf, cols - 1, recv_sem.at[3])
    total = jnp.sum(ybuf[...], axis=0)
    cor = [inc[f] * total[f : f + 1] for f in range(4)]
    for f in range(4):
        cpad[f : f + 1, :] = cor[f]
    rz += float(fb) * (means[1] * cor[1] + means[3] * cor[3])
    for f in range(4):
        kc = gp[f] * 2.0
        for g in range(4):
            kc += ke[f][:, g : g + 1] * cor[g]
        pp += cor[f] * kc
        pq += cor[f] * hq[f]
    a1send[0:1, :] = rz
    a1send[1:2, :] = pp
    a1send[2:3, :] = 2.0 * pq
    a1send[3:4, :] = qq
    others(layers, lay, lambda l: send(a1send, a1buf.at[lay], 4, l, col))
    a1buf[pl.ds(lay, 1)] = a1send[...][None]

    change = mm(sqe[:, 128:256], cpad[...])
    for f in range(4):
        hsrc[2, f] = spv[face(f), :] + change[f * fb : (f + 1) * fb]
    halo(2, 1)
    halo(2, 0)
    for f in range(4):
        pd[face(f), :] = pd[face(f), :] + cor[f]
    wait_all(hdst.at[1], 4, hrecv_sem.at[1])
    for f in range(4):
        sqe[face(f), 0:128] = assembled(1, hsrc[1, f], f)
    loads[5].wait()

    wait_all(a1buf, layers - 1, recv_sem.at[4])
    a2send[...] = jnp.sum(a1buf[...], axis=0)
    others(cols, col, lambda c: send(a2send, a2buf.at[col], 5, lay, c))
    a2buf[pl.ds(col, 1)] = a2send[...][None]
    wait_all(hdst.at[2], 4, hrecv_sem.at[2])
    for f in range(4):
        spv[face(f), :] = assembled(2, hsrc[2, f], f)
    wait_all(rbuf, layers - 1, send_sem.at[0])
    wait_all(cbuf_a, cols - 1, send_sem.at[1])
    wait_all(cbuf_b, cols, send_sem.at[2])
    wait_all(ybuf, cols - 1, send_sem.at[3])
    wait_all(a1buf, layers - 1, send_sem.at[4])
    for i in range(3):
        wait_all(hsrc.at[i], 4, hsend_sem.at[i])

    wait_all(a2buf, cols - 1, recv_sem.at[5])
    sums = jnp.sum(a2buf[...], axis=0)
    rz_all = sums[0:1]
    beta = rz_all / prz_ref[...]
    curvature = sums[1:2] + beta * (sums[2:3] + beta * sums[3:4])
    alpha = rz_all / curvature
    rz_ref[...] = rz_all
    for f in range(4):
        direction = pd[face(f), :] + beta * qv[face(f), :]
        out_ref[2, f] = direction
        out_ref[0, f] = xv[face(f), :] + alpha * direction
        image = spv[face(f), :] + beta * sqe[face(f), 0:128]
        out_ref[1, f] = rv[face(f), :] - alpha * image
    wait_all(a2buf, cols - 1, send_sem.at[5])


def spread(all_ref, rz_in, x_ref, r_ref, d_ref, rz_ref, sem):
    parts = [(all_ref.at[i], ref) for i, ref in enumerate((x_ref, r_ref, d_ref))]
    parts.append((rz_in, rz_ref))
    copies = [pltpu.make_async_copy(src, dst, sem.at[i]) for i, (src, dst) in enumerate(parts)]
    for one in copies:
        one.start()
    for one in copies:
        one.wait()


def solution(mesh):
    layers, cols = mesh.shape["layer"], mesh.shape["col"]

    def per_device(
        iterate,
        residual_in,
        direction_in,
        previous_rz,
        local_schur,
        local_inverse,
        coarse_inverse,
        face_included,
    ):
        _, _, _, fb, rhs = iterate.shape
        nb = 4 * fb
        nco = coarse_inverse.shape[1]
        lanes = min(128, nco)
        f32 = jnp.float32
        flat = [v.reshape(nb, rhs) for v in (iterate, residual_in, direction_in)]
        hbm = pl.BlockSpec(memory_space=pltpu.HBM)
        vmem = pl.BlockSpec(memory_space=pltpu.VMEM)
        field = jax.ShapeDtypeStruct((4, fb, rhs), f32)
        scalar = jax.ShapeDtypeStruct((1, rhs), f32)
        vec = pltpu.VMEM((nb, rhs), f32)
        mat = pltpu.VMEM((nb, nb), f32)
        wide = pltpu.VMEM((nb, 256), f32)
        every, rz = pl.pallas_call(
            functools.partial(kernel, layers, cols),
            out_shape=(pltpu.VMEM((3, 4, fb, rhs), f32), pltpu.VMEM((1, rhs), f32)),
            in_specs=[pl.BlockSpec(memory_space=pltpu.SMEM), vmem] + [hbm] * 6,
            out_specs=(vmem, vmem),
            scratch_shapes=[
                vec,
                vec,
                vec,
                mat,
                mat,
                pltpu.VMEM((2, nco), f32),
                pltpu.VMEM((2, 128, lanes), f32),
                pltpu.VMEM((cols, 4, 128), f32),
                pltpu.VMEM((cols, 4, 128), f32),
                pltpu.VMEM((cols, 4, 128), f32),
                pltpu.VMEM((2, 4 * cols, 128), f32),
                wide,
                wide,
                vec,
                vec,
                pltpu.VMEM((3, 4, fb, rhs), f32),
                pltpu.VMEM((3, 4, fb, rhs), f32),
                pltpu.VMEM((2, rhs), f32),
                pltpu.VMEM((layers, 2, rhs), f32),
                pltpu.VMEM((128, rhs), f32),
                pltpu.VMEM((cols, 4, rhs), f32),
                pltpu.VMEM((cols, 4, rhs), f32),
                pltpu.VMEM((128, rhs), f32),
                pltpu.VMEM((4, rhs), f32),
                pltpu.VMEM((layers, 4, rhs), f32),
                pltpu.VMEM((4, rhs), f32),
                pltpu.VMEM((cols, 4, rhs), f32),
                pltpu.SemaphoreType.DMA((6,)),
                pltpu.SemaphoreType.DMA((6,)),
                pltpu.SemaphoreType.DMA((6,)),
                pltpu.SemaphoreType.DMA((3,)),
                pltpu.SemaphoreType.DMA((3,)),
            ],
            compiler_params=pltpu.CompilerParams(
                collective_id=0, has_side_effects=True, vmem_limit_bytes=VMEM_LIMIT
            ),
        )(
            face_included.reshape(4),
            previous_rz.reshape(1, rhs),
            *flat,
            local_schur.reshape(nb, nb),
            local_inverse.reshape(nb, nb),
            coarse_inverse,
        )
        xo, ro, do, rz = pl.pallas_call(
            spread,
            out_shape=(field, field, field, scalar),
            in_specs=[vmem] * 2,
            out_specs=(hbm, hbm, hbm, hbm),
            scratch_shapes=[pltpu.SemaphoreType.DMA((4,))],
            compiler_params=pltpu.CompilerParams(vmem_limit_bytes=1024 * 1024),
        )(pltpu.with_memory_space_constraint(every, pltpu.VMEM), pltpu.with_memory_space_constraint(rz, pltpu.VMEM))
        shape = iterate.shape
        return xo.reshape(shape), ro.reshape(shape), do.reshape(shape), rz.reshape(rhs)

    placed = (
        P("layer", "col", None, None, None),
        P("layer", "col", None, None, None),
        P("layer", "col", None, None, None),
        P(),
        P("layer", "col", None, None),
        P("layer", "col", None, None),
        P(("layer", "col"), None),
        P("layer", "col", None),
    )
    return jax.shard_map(
        per_device,
        mesh=mesh,
        in_specs=placed,
        out_specs=(
            P("layer", "col", None, None, None),
            P("layer", "col", None, None, None),
            P("layer", "col", None, None, None),
            P(),
        ),
        check_vma=False,
    )
```

time: 55 us -> 45.5 us (0.83)
  local copies, waits for them, and re-layouts: 8.6 us -> 0 us
  Pallas kernels: 45.4 us -> 44.7 us
    unnamed x20 -> x0, local copies, waits for them, and re-layouts: 8.6 us -> none
    pallas_call x1 -> x2, Pallas kernels: 45.4 us -> 44.7 us  [the longest x1 43.8 us: per_device(): pl.pallas_call(functools.partial(kernel, layers, cols), out_shape=(pltpu....]
where the time goes in v2:
time: 45.5 us; the launch traced here: 45.4 us
  Pallas kernels  44.7 us (98%)
  between operations  0.64 us (1%)
    pallas_call x1, Pallas kernels, per_device(): pl.pallas_call(functools.partial(kernel, layers, cols), out_shape=(pltpu....  43.8 us
    pallas_call x1, Pallas kernels, per_device(): pl.pallas_call(spread, out_shape=(field, field, field, scalar), in_specs=...  0.91 us

profile of v2, /device:TPU:1, one launch (start us, length us, event | category | flops | bytes accessed | tf_op | source)
XLA Modules:
  0.0 45.4 jit_solution(11289044260231503101)
XLA Ops:
  0.6 43.8 %shard_map.111 = (f32[3,4,128,128]{3,2,1,0:T(8,128)S(1)}, f32[1,128]{1,0:T(1,128)S(1)}) custom-call(s32[4]{0:T(128)} %bitcast.16, f32[1,128]{1,0:T(1,128)} %bitcast.17, f32[512,128]{1,0:T(8,128)} %bitcast.13, f32[512,128]{1,0:T(8,128)} %bitcast.14, f32[512,128]{1,0:T(8,128)} %bitcast.15, f32[512,512]{1,0:T(8,128)} %bitcast.11, f32[512,512]{1,0:T(8,128)} %bitcast.12, ...), custom_call_target="tpu_custom_call" | custom-call | tf_op jit(solution)/shard_map/pallas_call | solution.py:363
  44.4 0.9 %shard_map.112 = (f32[4,128,128]{2,1,0:T(8,128)}, f32[4,128,128]{2,1,0:T(8,128)}, f32[4,128,128]{2,1,0:T(8,128)}, f32[1,128]{1,0:T(1,128)}) custom-call(f32[3,4,128,128]{3,2,1,0:T(8,128)S(1)} %get-tuple-element.10.all_ref, f32[1,128]{1,0:T(1,128)S(1)} %get-tuple-element.11.rz_in), custom_call_target="tpu_custom_call" | custom-call | tf_op jit(solution)/shard_map/pallas_call | solution.py:413

commit v3 on v2

v3 whole, which is shorter than its diff:
```python
import functools
import jax
import jax.numpy as jnp
from jax import lax
from jax.experimental import pallas as pl
from jax.experimental.pallas import tpu as pltpu
from jax.sharding import PartitionSpec as P

MESH = pl.DeviceIdType.MESH
HIGH = lax.Precision.HIGHEST
VMEM_LIMIT = 60 * 1024 * 1024


def mm(a, b):
    return jnp.dot(a, b, precision=HIGH, preferred_element_type=jnp.float32)


def wait_all(ref, count, sem):
    part = ref.at[pl.ds(0, count)]
    pltpu.make_async_copy(part, part, sem).wait()


def kernel(
    layers,
    cols,
    inc_ref,
    prz_ref,
    x_hbm,
    r_hbm,
    q_hbm,
    s_hbm,
    m_hbm,
    c_hbm,
    out_ref,
    rz_ref,
    xv,
    rv,
    qv,
    sv,
    mv,
    cv,
    rhs,
    sqe,
    spv,
    pd,
    hsrc,
    hdst,
    rsend,
    rbuf,
    cbuf,
    zmat,
    ct,
    turned,
    rall,
    ksend,
    kbuf,
    csend,
    crecv,
    cpad,
    a2send,
    a2buf,
    ssend,
    srecv,
    in_sem,
    send_sem,
    recv_sem,
    hsend_sem,
    hrecv_sem,
):
    fb = xv.shape[0] // 4
    width = 2 * cols
    nco = cv.shape[1]
    lanes = min(128, nco)
    lay = lax.axis_index("layer")
    col = lax.axis_index("col")
    below = lax.rem(lay + layers - 1, layers)
    above = lax.rem(lay + 1, layers)
    left = lax.rem(col + cols - 1, cols)
    right = lax.rem(col + 1, cols)
    center = lay == 0
    outer = lay != 0

    def load(src, dst, i):
        return pltpu.make_async_copy(src, dst, in_sem.at[i])

    loads = [
        load(r_hbm, rv, 0),
        load(c_hbm, cv, 1),
        load(m_hbm, mv, 2),
        load(q_hbm, qv, 3),
        load(s_hbm, sv, 4),
        load(x_hbm, xv, 5),
    ]
    loads[0].start()

    barrier = pltpu.get_barrier_semaphore()

    def greet(l, c):
        pl.semaphore_signal(barrier, inc=1, device_id=(l, c), device_id_type=MESH)

    def others(n, me, act):
        def body(k, carry):
            act(lax.rem(me + k, n))
            return carry

        lax.fori_loop(1, n, body, 0)

    def send(src, dst, i, l, c):
        pltpu.make_async_remote_copy(
            src_ref=src,
            dst_ref=dst,
            send_sem=send_sem.at[i],
            recv_sem=recv_sem.at[i],
            device_id=(l, c),
            device_id_type=MESH,
        ).start()

    greet(below, col)
    greet(above, col)
    greet(lay, left)
    greet(lay, right)

    @pl.when(outer)
    def _():
        greet(0, col)

    for one in loads[1:]:
        one.start()

    @pl.when(center)
    def _():
        others(layers, lay, lambda l: greet(l, col))
        others(cols, col, lambda c: greet(lay, c))

    def face(f):
        return pl.ds(f * fb, fb)

    def halo(i):
        pairs = ((0, 1, below, col), (1, 0, above, col), (2, 3, lay, left), (3, 2, lay, right))
        for f, g, l, c in pairs:
            pltpu.make_async_remote_copy(
                src_ref=hsrc.at[i, f],
                dst_ref=hdst.at[i, g],
                send_sem=hsend_sem.at[i],
                recv_sem=hrecv_sem.at[i],
                device_id=(l, c),
                device_id_type=MESH,
            ).start()

    def assembled(i, own, f):
        got = hdst[i, f]
        if f == 0:
            got = jnp.where(lay > 0, got, 0.0)
        if f == 1:
            got = jnp.where(lay < layers - 1, got, 0.0)
        return own + got

    inc = [inc_ref[f].astype(jnp.float32) for f in range(4)]
    cpad[...] = jnp.zeros_like(cpad)

    loads[0].wait()
    means = []
    for f in range(4):
        res = inc[f] * rv[face(f), :]
        rv[face(f), :] = res
        mean = jnp.mean(res, axis=0, keepdims=True)
        means.append(mean)
        spv[face(f), :] = 0.5 * (res - mean)
    rsend[0:1, :] = means[1]
    rsend[1:2, :] = means[3]
    loads[1].wait()

    @pl.when(center)
    def _():
        zmat[3 * layers :, :] = jnp.zeros((zmat.shape[0] - 3 * layers, nco), jnp.float32)
        rbuf[0] = rsend[...]
        cbuf[0] = cv[...]
        pl.semaphore_wait(barrier, 4 + layers - 1 + cols - 1)

    @pl.when(outer)
    def _():
        pl.semaphore_wait(barrier, 5)
        send(rsend, rbuf.at[lay], 0, 0, col)
        send(cv, cbuf.at[lay], 1, 0, col)

    loads[2].wait()
    inner = mm(mv[...], spv[...])
    rz = jnp.zeros_like(means[0])
    for f in range(4):
        part = inner[f * fb : (f + 1) * fb]
        half = 0.5 * (inc[f] * (part - jnp.mean(part, axis=0, keepdims=True)))
        hsrc[0, f] = half
        rz += jnp.sum(rv[face(f), :] * half, axis=0, keepdims=True)
    halo(0)
    ksend[8:9, :] = rz

    loads[3].wait()
    lane = lax.broadcasted_iota(jnp.int32, (fb, 128), 1)
    for f in range(4):
        prev = inc[f] * qv[face(f), :]
        qv[face(f), :] = prev
        rhs[face(f), 0:128] = prev
        rhs[face(f), 128:256] = jnp.where(lane == f, inc[f], 0.0)
    loads[4].wait()
    sqe[...] = mm(sv[...], rhs[...])
    qq = jnp.zeros_like(rz)
    for f in range(4):
        sq = inc[f] * sqe[face(f), 0:128]
        se = inc[f] * sqe[face(f), 128:256]
        sqe[face(f), 128:256] = se
        hsrc[1, f] = sq
        qq += jnp.sum(qv[face(f), :] * sq, axis=0, keepdims=True)
        ksend[4 + f : 5 + f, :] = 2.0 * jnp.sum(sq, axis=0, keepdims=True)
        ksend[12 + f : 13 + f, :] = jnp.sum(se, axis=0, keepdims=True)
    halo(1)
    ksend[11:12, :] = qq

    @pl.when(center)
    def _():
        wait_all(rbuf, layers - 1, recv_sem.at[0])
        for l in range(layers):
            for g in range(2):
                rall[col, g * layers + l : g * layers + l + 1, :] = rbuf[l, g : g + 1, :]
        others(cols, col, lambda c: send(rall.at[col], rall.at[col], 2, 0, c))
        wait_all(cbuf, layers - 1, recv_sem.at[1])
        for l in range(layers):
            for g in range(2):
                zmat[g * layers + l : g * layers + l + 1, :] = cbuf[l, g : g + 1, :]
        mid = zmat.at[pl.ds(layers, layers)]
        send(mid, zmat.at[pl.ds(2 * layers, layers)], 7, 0, right)

    wait_all(hdst.at[0], 4, hrecv_sem.at[0])
    for f in range(4):
        pd[face(f), :] = assembled(0, hsrc[0, f], f)
    spv[...] = mm(sv[...], pd[...])
    pp = jnp.zeros_like(rz)
    pq = jnp.zeros_like(rz)
    for f in range(4):
        sp = inc[f] * spv[face(f), :]
        spv[face(f), :] = sp
        here = pd[face(f), :]
        pp += jnp.sum(here * sp, axis=0, keepdims=True)
        pq += jnp.sum(here * hsrc[1, f], axis=0, keepdims=True)
        ksend[f : f + 1, :] = 2.0 * jnp.sum(sp, axis=0, keepdims=True)
    ksend[9:10, :] = pp
    ksend[10:11, :] = 2.0 * pq

    @pl.when(outer)
    def _():
        send(ksend, kbuf.at[lay], 3, 0, col)

    @pl.when(center)
    def _():
        wait_all(zmat, layers, recv_sem.at[7])
        wait_all(zmat, layers, send_sem.at[7])
        for j in range(nco // lanes):
            ct[j * lanes : (j + 1) * lanes, :] = zmat[:, j * lanes : (j + 1) * lanes].T
        for c in range(cols):
            for g in range(2):
                at = (2 * c + g) * layers
                turned[at : at + layers, :] = ct[pl.ds(2 * c + g, layers, stride=width), :]
        for j in range(nco // lanes):
            zmat[:, j * lanes : (j + 1) * lanes] = turned[j * lanes : (j + 1) * lanes, :].T

    wait_all(hdst.at[1], 4, hrecv_sem.at[1])
    for f in range(4):
        sqe[face(f), 0:128] = assembled(1, hsrc[1, f], f)
    loads[5].wait()

    @pl.when(center)
    def _():
        kbuf[0] = ksend[...]
        wait_all(rall, cols - 1, recv_sem.at[2])
        total = mm(zmat[0 : 3 * layers, :], rall[...].reshape(nco, rall.shape[2]))
        for l in range(layers):
            low = (l + layers - 1) % layers
            csend[l, 0:1, :] = total[low : low + 1]
            csend[l, 1:2, :] = total[l : l + 1]
            csend[l, 2:3, :] = total[2 * layers + l : 2 * layers + l + 1]
            csend[l, 3:4, :] = total[layers + l : layers + l + 1]
        others(layers, lay, lambda l: send(csend.at[l], crecv, 4, l, col))
        wait_all(kbuf, layers - 1, recv_sem.at[3])
        base = jnp.zeros_like(a2send)
        quad = jnp.zeros_like(a2send)
        cross = jnp.zeros_like(a2send)
        work = jnp.zeros((1, a2send.shape[1]), jnp.float32)
        for l in range(layers):
            cor = csend[l]
            mixed = kbuf[l, 0:4, :]
            block = kbuf[l, 12:16, :]
            for g in range(4):
                mixed += block[:, g : g + 1] * cor[g : g + 1]
            quad += cor * mixed
            cross += cor * kbuf[l, 4:8, :]
            base += kbuf[l, 8:12, :]
            work += rbuf[l, 0:1, :] * cor[1:2] + rbuf[l, 1:2, :] * cor[3:4]
        a2send[0:1, :] = base[0:1] + float(fb) * work
        a2send[1:2, :] = base[1:2] + jnp.sum(quad, axis=0, keepdims=True)
        a2send[2:3, :] = base[2:3] + jnp.sum(cross, axis=0, keepdims=True)
        a2send[3:4, :] = base[3:4]
        others(cols, col, lambda c: send(a2send, a2buf.at[col], 5, lay, c))
        a2buf[pl.ds(col, 1)] = a2send[...][None]
        crecv[...] = csend[0]

    @pl.when(outer)
    def _():
        wait_all(crecv, 4, recv_sem.at[4])

    cor = [inc[f] * crecv[f : f + 1, :] for f in range(4)]
    for f in range(4):
        cpad[f : f + 1, :] = cor[f]
    change = mm(sqe[:, 128:256], cpad[...])
    for f in range(4):
        hsrc[2, f] = spv[face(f), :] + change[f * fb : (f + 1) * fb]
    halo(2)
    for f in range(4):
        pd[face(f), :] = pd[face(f), :] + cor[f]

    @pl.when(center)
    def _():
        wait_all(a2buf, cols - 1, recv_sem.at[5])
        ssend[...] = jnp.sum(a2buf[...], axis=0)
        others(layers, lay, lambda l: send(ssend, srecv, 6, l, col))
        srecv[...] = ssend[...]

    wait_all(hdst.at[2], 4, hrecv_sem.at[2])
    for f in range(4):
        spv[face(f), :] = assembled(2, hsrc[2, f], f)

    @pl.when(outer)
    def _():
        wait_all(srecv, 4, recv_sem.at[6])

    sums = srecv[...]
    rz_all = sums[0:1]
    beta = rz_all / prz_ref[...]
    curvature = sums[1:2] + beta * (sums[2:3] + beta * sums[3:4])
    alpha = rz_all / curvature
    rz_ref[...] = rz_all
    for f in range(4):
        direction = pd[face(f), :] + beta * qv[face(f), :]
        out_ref[2, f] = direction
        out_ref[0, f] = xv[face(f), :] + alpha * direction
        image = spv[face(f), :] + beta * sqe[face(f), 0:128]
        out_ref[1, f] = rv[face(f), :] - alpha * image

    for i in range(3):
        wait_all(hsrc.at[i], 4, hsend_sem.at[i])

    @pl.when(center)
    def _():
        wait_all(rall, cols - 1, send_sem.at[2])
        wait_all(csend, layers - 1, send_sem.at[4])
        wait_all(a2buf, cols - 1, send_sem.at[5])
        wait_all(csend, layers - 1, send_sem.at[6])

    @pl.when(outer)
    def _():
        wait_all(rsend, 2, send_sem.at[0])
        wait_all(cv, 2, send_sem.at[1])
        wait_all(ksend, 16, send_sem.at[3])


def spread(all_ref, rz_in, x_ref, r_ref, d_ref, rz_ref, sem):
    parts = [(all_ref.at[i], ref) for i, ref in enumerate((x_ref, r_ref, d_ref))]
    parts.append((rz_in, rz_ref))
    copies = [pltpu.make_async_copy(src, dst, sem.at[i]) for i, (src, dst) in enumerate(parts)]
    for one in copies:
        one.start()
    for one in copies:
        one.wait()


def solution(mesh):
    layers, cols = mesh.shape["layer"], mesh.shape["col"]

    def per_device(
        iterate,
        residual_in,
        direction_in,
        previous_rz,
        local_schur,
        local_inverse,
        coarse_inverse,
        face_included,
    ):
        _, _, _, fb, rhs = iterate.shape
        nb = 4 * fb
        nco = coarse_inverse.shape[1]
        f32 = jnp.float32
        flat = [v.reshape(nb, rhs) for v in (iterate, residual_in, direction_in)]
        hbm = pl.BlockSpec(memory_space=pltpu.HBM)
        vmem = pl.BlockSpec(memory_space=pltpu.VMEM)
        field = jax.ShapeDtypeStruct((4, fb, rhs), f32)
        scalar = jax.ShapeDtypeStruct((1, rhs), f32)
        vec = pltpu.VMEM((nb, rhs), f32)
        mat = pltpu.VMEM((nb, nb), f32)
        wide = pltpu.VMEM((nb, 256), f32)
        every, rz = pl.pallas_call(
            functools.partial(kernel, layers, cols),
            out_shape=(pltpu.VMEM((3, 4, fb, rhs), f32), pltpu.VMEM((1, rhs), f32)),
            in_specs=[pl.BlockSpec(memory_space=pltpu.SMEM), vmem] + [hbm] * 6,
            out_specs=(vmem, vmem),
            scratch_shapes=[
                vec,
                vec,
                vec,
                mat,
                mat,
                pltpu.VMEM((2, nco), f32),
                wide,
                wide,
                vec,
                vec,
                pltpu.VMEM((3, 4, fb, rhs), f32),
                pltpu.VMEM((3, 4, fb, rhs), f32),
                pltpu.VMEM((2, rhs), f32),
                pltpu.VMEM((layers, 2, rhs), f32),
                pltpu.VMEM((layers, 2, nco), f32),
                pltpu.VMEM((128, nco), f32),
                pltpu.VMEM((nco, 128), f32),
                pltpu.VMEM((nco, 128), f32),
                pltpu.VMEM((cols, 2 * layers, rhs), f32),
                pltpu.VMEM((16, rhs), f32),
                pltpu.VMEM((layers, 16, rhs), f32),
                pltpu.VMEM((layers, 4, rhs), f32),
                pltpu.VMEM((4, rhs), f32),
                pltpu.VMEM((128, rhs), f32),
                pltpu.VMEM((4, rhs), f32),
                pltpu.VMEM((cols, 4, rhs), f32),
                pltpu.VMEM((4, rhs), f32),
                pltpu.VMEM((4, rhs), f32),
                pltpu.SemaphoreType.DMA((6,)),
                pltpu.SemaphoreType.DMA((8,)),
                pltpu.SemaphoreType.DMA((8,)),
                pltpu.SemaphoreType.DMA((3,)),
                pltpu.SemaphoreType.DMA((3,)),
            ],
            compiler_params=pltpu.CompilerParams(
                collective_id=0, has_side_effects=True, vmem_limit_bytes=VMEM_LIMIT
            ),
        )(
            face_included.reshape(4),
            previous_rz.reshape(1, rhs),
            *flat,
            local_schur.reshape(nb, nb),
            local_inverse.reshape(nb, nb),
            coarse_inverse,
        )
        xo, ro, do, rz = pl.pallas_call(
            spread,
            out_shape=(field, field, field, scalar),
            in_specs=[vmem] * 2,
            out_specs=(hbm, hbm, hbm, hbm),
            scratch_shapes=[pltpu.SemaphoreType.DMA((4,))],
            compiler_params=pltpu.CompilerParams(vmem_limit_bytes=1024 * 1024),
        )(pltpu.with_memory_space_constraint(every, pltpu.VMEM), pltpu.with_memory_space_constraint(rz, pltpu.VMEM))
        shape = iterate.shape
        return xo.reshape(shape), ro.reshape(shape), do.reshape(shape), rz.reshape(rhs)

    placed = (
        P("layer", "col", None, None, None),
        P("layer", "col", None, None, None),
        P("layer", "col", None, None, None),
        P(),
        P("layer", "col", None, None),
        P("layer", "col", None, None),
        P(("layer", "col"), None),
        P("layer", "col", None),
    )
    return jax.shard_map(
        per_device,
        mesh=mesh,
        in_specs=placed,
        out_specs=(
            P("layer", "col", None, None, None),
            P("layer", "col", None, None, None),
            P("layer", "col", None, None, None),
            P(),
        ),
        check_vma=False,
    )
```

time: 45.5 us -> 39.7 us (0.87)
  the two profiles are of different devices: /device:TPU:1 before, /device:TPU:6 now
where the time goes in v3:
time: 39.7 us; the launch traced here: 39.6 us
  Pallas kernels  39 us (98%)
  between operations  0.64 us (2%)
    pallas_call x1, Pallas kernels, per_device(): pl.pallas_call(functools.partial(kernel, layers, cols), out_shape=(pltpu....  38 us
    pallas_call x1, Pallas kernels, per_device(): pl.pallas_call(spread, out_shape=(field, field, field, scalar), in_specs=...  0.91 us

profile of v3, /device:TPU:6, one launch (start us, length us, event | category | flops | bytes accessed | tf_op | source)
XLA Modules:
  0.0 39.6 jit_solution(17063233469660121372)
XLA Ops:
  0.6 38.0 %shard_map.111 = (f32[3,4,128,128]{3,2,1,0:T(8,128)S(1)}, f32[1,128]{1,0:T(1,128)S(1)}) custom-call(s32[4]{0:T(128)} %bitcast.16, f32[1,128]{1,0:T(1,128)} %bitcast.17, f32[512,128]{1,0:T(8,128)} %bitcast.13, f32[512,128]{1,0:T(8,128)} %bitcast.14, f32[512,128]{1,0:T(8,128)} %bitcast.15, f32[512,512]{1,0:T(8,128)} %bitcast.11, f32[512,512]{1,0:T(8,128)} %bitcast.12, ...), custom_call_target="tpu_custom_call" | custom-call | tf_op jit(solution)/shard_map/pallas_call | solution.py:399
  38.7 0.9 %shard_map.112 = (f32[4,128,128]{2,1,0:T(8,128)}, f32[4,128,128]{2,1,0:T(8,128)}, f32[4,128,128]{2,1,0:T(8,128)}, f32[1,128]{1,0:T(1,128)}) custom-call(f32[3,4,128,128]{3,2,1,0:T(8,128)S(1)} %get-tuple-element.10.all_ref, f32[1,128]{1,0:T(1,128)S(1)} %get-tuple-element.11.rz_in), custom_call_target="tpu_custom_call" | custom-call | tf_op jit(solution)/shard_map/pallas_call | solution.py:450

commit v4 on v3

--- a/solution.py
+++ b/solution.py
@@ -52,6 +52,7 @@
     ct,
     turned,
     rall,
+    rlate,
     ksend,
     kbuf,
     csend,
@@ -79,19 +80,32 @@
     right = lax.rem(col + 1, cols)
     center = lay == 0
     outer = lay != 0
+    top = lay == layers - 1
+    inside = outer & (lay != layers - 1)
+    first, last = max(1, layers // 2 - 1), min(layers, layers // 2 + 3)
+    late = list(range(first, last))
+    early = [l for l in range(layers) if l not in late]
+    far = (lay >= first) & (lay < last)
+
+    def face(f):
+        return pl.ds(f * fb, fb)
 
     def load(src, dst, i):
         return pltpu.make_async_copy(src, dst, in_sem.at[i])
 
     loads = [
-        load(r_hbm, rv, 0),
+        load(r_hbm.at[1], rv.at[face(1), :], 0),
         load(c_hbm, cv, 1),
         load(m_hbm, mv, 2),
         load(q_hbm, qv, 3),
         load(s_hbm, sv, 4),
         load(x_hbm, xv, 5),
+        load(r_hbm.at[3], rv.at[face(3), :], 6),
+        load(r_hbm.at[0], rv.at[face(0), :], 7),
+        load(r_hbm.at[2], rv.at[face(2), :], 8),
     ]
     loads[0].start()
+    loads[6].start()
 
     barrier = pltpu.get_barrier_semaphore()
 
@@ -115,29 +129,20 @@
             device_id_type=MESH,
         ).start()
 
-    greet(below, col)
-    greet(above, col)
     greet(lay, left)
     greet(lay, right)
-
-    @pl.when(outer)
-    def _():
-        greet(0, col)
-
-    for one in loads[1:]:
-        one.start()
+    pl.when(outer)(lambda: greet(below, col))
+    pl.when(jnp.logical_not(top))(lambda: greet(above, col))
+    for i in (7, 8, 1, 2, 3, 4, 5):
+        loads[i].start()
 
     @pl.when(center)
     def _():
         others(layers, lay, lambda l: greet(l, col))
         others(cols, col, lambda c: greet(lay, c))
 
-    def face(f):
-        return pl.ds(f * fb, fb)
-
     def halo(i):
-        pairs = ((0, 1, below, col), (1, 0, above, col), (2, 3, lay, left), (3, 2, lay, right))
-        for f, g, l, c in pairs:
+        def one(f, g, l, c):
             pltpu.make_async_remote_copy(
                 src_ref=hsrc.at[i, f],
                 dst_ref=hdst.at[i, g],
@@ -147,6 +152,15 @@
                 device_id_type=MESH,
             ).start()
 
+        pl.when(outer)(lambda: one(0, 1, below, col))
+        pl.when(jnp.logical_not(top))(lambda: one(1, 0, above, col))
+        one(2, 3, lay, left)
+        one(3, 2, lay, right)
+
+    def halo_wait(i, sem):
+        pl.when(inside)(lambda: wait_all(hdst.at[i], 4, sem.at[i]))
+        pl.when(jnp.logical_not(inside))(lambda: wait_all(hdst.at[i], 3, sem.at[i]))
+
     def assembled(i, own, f):
         got = hdst[i, f]
         if f == 0:
@@ -158,31 +172,44 @@
     inc = [inc_ref[f].astype(jnp.float32) for f in range(4)]
     cpad[...] = jnp.zeros_like(cpad)
 
-    loads[0].wait()
-    means = []
-    for f in range(4):
+    means = {}
+
+    def average(f, i):
+        loads[i].wait()
         res = inc[f] * rv[face(f), :]
         rv[face(f), :] = res
-        mean = jnp.mean(res, axis=0, keepdims=True)
-        means.append(mean)
-        spv[face(f), :] = 0.5 * (res - mean)
+        means[f] = jnp.mean(res, axis=0, keepdims=True)
+        spv[face(f), :] = 0.5 * (res - means[f])
+
+    average(1, 0)
+    average(3, 6)
     rsend[0:1, :] = means[1]
     rsend[1:2, :] = means[3]
-    loads[1].wait()
 
     @pl.when(center)
     def _():
         zmat[3 * layers :, :] = jnp.zeros((zmat.shape[0] - 3 * layers, nco), jnp.float32)
         rbuf[0] = rsend[...]
+        loads[1].wait()
         cbuf[0] = cv[...]
-        pl.semaphore_wait(barrier, 4 + layers - 1 + cols - 1)
-
     @pl.when(outer)
     def _():
-        pl.semaphore_wait(barrier, 5)
-        send(rsend, rbuf.at[lay], 0, 0, col)
+        pl.when(top)(lambda: pl.semaphore_wait(barrier, 4))
+        pl.when(inside)(lambda: pl.semaphore_wait(barrier, 5))
+
+        @pl.when(far)
+        def _():
+            send(rsend, rbuf.at[lay], 8, 0, col)
+
+        @pl.when(jnp.logical_not(far))
+        def _():
+            send(rsend, rbuf.at[lay], 0, 0, col)
+
+        loads[1].wait()
         send(cv, cbuf.at[lay], 1, 0, col)
 
+    average(0, 7)
+    average(2, 8)
     loads[2].wait()
     inner = mm(mv[...], spv[...])
     rz = jnp.zeros_like(means[0])
@@ -191,7 +218,7 @@
         half = 0.5 * (inc[f] * (part - jnp.mean(part, axis=0, keepdims=True)))
         hsrc[0, f] = half
         rz += jnp.sum(rv[face(f), :] * half, axis=0, keepdims=True)
-    halo(0)
+    pl.when(outer)(lambda: halo(0))
     ksend[8:9, :] = rz
 
     loads[3].wait()
@@ -212,16 +239,26 @@
         qq += jnp.sum(qv[face(f), :] * sq, axis=0, keepdims=True)
         ksend[4 + f : 5 + f, :] = 2.0 * jnp.sum(sq, axis=0, keepdims=True)
         ksend[12 + f : 13 + f, :] = jnp.sum(se, axis=0, keepdims=True)
-    halo(1)
+    pl.when(outer)(lambda: halo(1))
     ksend[11:12, :] = qq
 
     @pl.when(center)
     def _():
-        wait_all(rbuf, layers - 1, recv_sem.at[0])
-        for l in range(layers):
+        pl.semaphore_wait(barrier, 3 + cols - 1)
+        halo(0)
+        halo(1)
+        wait_all(rbuf, len(early) - 1, recv_sem.at[0])
+        for i, l in enumerate(early):
             for g in range(2):
-                rall[col, g * layers + l : g * layers + l + 1, :] = rbuf[l, g : g + 1, :]
+                at = g * len(early) + i
+                rall[col, at : at + 1, :] = rbuf[l, g : g + 1, :]
         others(cols, col, lambda c: send(rall.at[col], rall.at[col], 2, 0, c))
+        wait_all(rbuf, len(late), recv_sem.at[8])
+        for i, l in enumerate(late):
+            for g in range(2):
+                at = g * len(late) + i
+                rlate[col, at : at + 1, :] = rbuf[l, g : g + 1, :]
+        others(cols, col, lambda c: send(rlate.at[col], rlate.at[col], 9, 0, c))
         wait_all(cbuf, layers - 1, recv_sem.at[1])
         for l in range(layers):
             for g in range(2):
@@ -229,7 +266,7 @@
         mid = zmat.at[pl.ds(layers, layers)]
         send(mid, zmat.at[pl.ds(2 * layers, layers)], 7, 0, right)
 
-    wait_all(hdst.at[0], 4, hrecv_sem.at[0])
+    halo_wait(0, hrecv_sem)
     for f in range(4):
         pd[face(f), :] = assembled(0, hsrc[0, f], f)
     spv[...] = mm(sv[...], pd[...])
@@ -257,12 +294,20 @@
             ct[j * lanes : (j + 1) * lanes, :] = zmat[:, j * lanes : (j + 1) * lanes].T
         for c in range(cols):
             for g in range(2):
-                at = (2 * c + g) * layers
-                turned[at : at + layers, :] = ct[pl.ds(2 * c + g, layers, stride=width), :]
+                at = (2 * c + g) * len(early)
+                end = 2 * cols * len(early) + (2 * c + g) * len(late)
+                for src, dst, n in (
+                    (0, at, first),
+                    (last, at + first, layers - last),
+                    (first, end, len(late)),
+                ):
+                    if n:
+                        rows = ct[pl.ds(src * width + 2 * c + g, n, stride=width), :]
+                        turned[dst : dst + n, :] = rows
         for j in range(nco // lanes):
             zmat[:, j * lanes : (j + 1) * lanes] = turned[j * lanes : (j + 1) * lanes, :].T
 
-    wait_all(hdst.at[1], 4, hrecv_sem.at[1])
+    halo_wait(1, hrecv_sem)
     for f in range(4):
         sqe[face(f), 0:128] = assembled(1, hsrc[1, f], f)
     loads[5].wait()
@@ -271,7 +316,11 @@
     def _():
         kbuf[0] = ksend[...]
         wait_all(rall, cols - 1, recv_sem.at[2])
-        total = mm(zmat[0 : 3 * layers, :], rall[...].reshape(nco, rall.shape[2]))
+        cut = 2 * cols * len(early)
+        total = mm(zmat[0 : 3 * layers, 0:cut], rall[...].reshape(cut, rall.shape[2]))
+        wait_all(rlate, cols - 1, recv_sem.at[9])
+        rest = rlate[...].reshape(nco - cut, rall.shape[2])
+        total += mm(zmat[0 : 3 * layers, cut:nco], rest)
         for l in range(layers):
             low = (l + layers - 1) % layers
             csend[l, 0:1, :] = total[low : low + 1]
@@ -323,7 +372,7 @@
         others(layers, lay, lambda l: send(ssend, srecv, 6, l, col))
         srecv[...] = ssend[...]
 
-    wait_all(hdst.at[2], 4, hrecv_sem.at[2])
+    halo_wait(2, hrecv_sem)
     for f in range(4):
         spv[face(f), :] = assembled(2, hsrc[2, f], f)
 
@@ -345,18 +394,20 @@
         out_ref[1, f] = rv[face(f), :] - alpha * image
 
     for i in range(3):
-        wait_all(hsrc.at[i], 4, hsend_sem.at[i])
+        halo_wait(i, hsend_sem)
 
     @pl.when(center)
     def _():
         wait_all(rall, cols - 1, send_sem.at[2])
+        wait_all(rlate, cols - 1, send_sem.at[9])
         wait_all(csend, layers - 1, send_sem.at[4])
         wait_all(a2buf, cols - 1, send_sem.at[5])
         wait_all(csend, layers - 1, send_sem.at[6])
 
     @pl.when(outer)
     def _():
-        wait_all(rsend, 2, send_sem.at[0])
+        pl.when(far)(lambda: wait_all(rsend, 2, send_sem.at[8]))
+        pl.when(jnp.logical_not(far))(lambda: wait_all(rsend, 2, send_sem.at[0]))
         wait_all(cv, 2, send_sem.at[1])
         wait_all(ksend, 16, send_sem.at[3])
 
@@ -387,8 +438,9 @@
         _, _, _, fb, rhs = iterate.shape
         nb = 4 * fb
         nco = coarse_inverse.shape[1]
+        n_late = min(layers, layers // 2 + 3) - max(1, layers // 2 - 1)
         f32 = jnp.float32
-        flat = [v.reshape(nb, rhs) for v in (iterate, residual_in, direction_in)]
+        x, q = iterate.reshape(nb, rhs), direction_in.reshape(nb, rhs)
         hbm = pl.BlockSpec(memory_space=pltpu.HBM)
         vmem = pl.BlockSpec(memory_space=pltpu.VMEM)
         field = jax.ShapeDtypeStruct((4, fb, rhs), f32)
@@ -420,7 +472,8 @@
                 pltpu.VMEM((128, nco), f32),
                 pltpu.VMEM((nco, 128), f32),
                 pltpu.VMEM((nco, 128), f32),
-                pltpu.VMEM((cols, 2 * layers, rhs), f32),
+                pltpu.VMEM((cols, 2 * (layers - n_late), rhs), f32),
+                pltpu.VMEM((cols, 2 * n_late, rhs), f32),
                 pltpu.VMEM((16, rhs), f32),
                 pltpu.VMEM((layers, 16, rhs), f32),
                 pltpu.VMEM((layers, 4, rhs), f32),
@@ -430,9 +483,9 @@
                 pltpu.VMEM((cols, 4, rhs), f32),
                 pltpu.VMEM((4, rhs), f32),
                 pltpu.VMEM((4, rhs), f32),
-                pltpu.SemaphoreType.DMA((6,)),
-                pltpu.SemaphoreType.DMA((8,)),
-                pltpu.SemaphoreType.DMA((8,)),
+                pltpu.SemaphoreType.DMA((9,)),
+                pltpu.SemaphoreType.DMA((10,)),
+                pltpu.SemaphoreType.DMA((10,)),
                 pltpu.SemaphoreType.DMA((3,)),
                 pltpu.SemaphoreType.DMA((3,)),
             ],
@@ -442,7 +495,9 @@
         )(
             face_included.reshape(4),
             previous_rz.reshape(1, rhs),
-            *flat,
+            x,
+            residual_in.reshape(4, fb, rhs),
+            q,
             local_schur.reshape(nb, nb),
             local_inverse.reshape(nb, nb),
             coarse_inverse,

time: 39.7 us -> 37 us (0.932)
  the two profiles are of different devices: /device:TPU:6 before, /device:TPU:1 now
where the time goes in v4:
time: 37 us; the launch traced here: 36.8 us
  Pallas kernels  36.2 us (98%)
  between operations  0.64 us (2%)
    pallas_call x1, Pallas kernels, per_device(): pl.pallas_call(functools.partial(kernel, layers, cols), out_shape=(pltpu....  35.3 us
    pallas_call x1, Pallas kernels, per_device(): pl.pallas_call(spread, out_shape=(field, field, field, scalar), in_specs=...  0.91 us

profile of v4, /device:TPU:1, one launch (start us, length us, event | category | flops | bytes accessed | tf_op | source)
XLA Modules:
  0.0 36.8 jit_solution(10294755641428629782)
XLA Ops:
  0.6 35.3 %shard_map.111 = (f32[3,4,128,128]{3,2,1,0:T(8,128)S(1)}, f32[1,128]{1,0:T(1,128)S(1)}) custom-call(s32[4]{0:T(128)} %bitcast.16, f32[1,128]{1,0:T(1,128)} %bitcast.17, f32[512,128]{1,0:T(8,128)} %bitcast.13, f32[4,128,128]{2,1,0:T(8,128)} %bitcast.14, f32[512,128]{1,0:T(8,128)} %bitcast.15, f32[512,512]{1,0:T(8,128)} %bitcast.11, f32[512,512]{1,0:T(8,128)} %bitcast.12, ...), custom_call_target="tpu_custom_call" | custom-call | tf_op jit(solution)/shard_map/pallas_call | solution.py:451
  35.9 0.9 %shard_map.112 = (f32[4,128,128]{2,1,0:T(8,128)}, f32[4,128,128]{2,1,0:T(8,128)}, f32[4,128,128]{2,1,0:T(8,128)}, f32[1,128]{1,0:T(1,128)}) custom-call(f32[3,4,128,128]{3,2,1,0:T(8,128)S(1)} %get-tuple-element.10.all_ref, f32[1,128]{1,0:T(1,128)S(1)} %get-tuple-element.11.rz_in), custom_call_target="tpu_custom_call" | custom-call | tf_op jit(solution)/shard_map/pallas_call | solution.py:505

commit v5 on v4

--- a/solution.py
+++ b/solution.py
@@ -47,6 +47,7 @@
     hdst,
     rsend,
     rbuf,
+    rfar,
     cbuf,
     zmat,
     ct,
@@ -79,12 +80,15 @@
     left = lax.rem(col + cols - 1, cols)
     right = lax.rem(col + 1, cols)
     center = lay == 0
+    pair, core = col // 2, lax.rem(col, 2)
+    twin = 2 * pair + 1 - core
     outer = lay != 0
     top = lay == layers - 1
     inside = outer & (lay != layers - 1)
     first, last = max(1, layers // 2 - 1), min(layers, layers // 2 + 3)
     late = list(range(first, last))
     early = [l for l in range(layers) if l not in late]
+    near = min(4, layers)
     far = (lay >= first) & (lay < last)
 
     def face(f):
@@ -119,6 +123,15 @@
 
         lax.fori_loop(1, n, body, 0)
 
+    def first_ones(n, me, heads, act):
+        for h in range(heads):
+            pl.when(me != h)(functools.partial(act, h))
+
+        def rest(p):
+            pl.when(p >= heads)(lambda: act(p))
+
+        others(n, me, rest)
+
     def send(src, dst, i, l, c):
         pltpu.make_async_remote_copy(
             src_ref=src,
@@ -139,6 +152,7 @@
     @pl.when(center)
     def _():
         others(layers, lay, lambda l: greet(l, col))
+        others(layers, lay, lambda l: greet(l, twin))
         others(cols, col, lambda c: greet(lay, c))
 
     def halo(i):
@@ -194,12 +208,13 @@
         cbuf[0] = cv[...]
     @pl.when(outer)
     def _():
-        pl.when(top)(lambda: pl.semaphore_wait(barrier, 4))
-        pl.when(inside)(lambda: pl.semaphore_wait(barrier, 5))
+        pl.when(top)(lambda: pl.semaphore_wait(barrier, 5))
+        pl.when(inside)(lambda: pl.semaphore_wait(barrier, 6))
 
         @pl.when(far)
         def _():
-            send(rsend, rbuf.at[lay], 8, 0, col)
+            send(rsend, rfar.at[core, lay - first], 8, 0, col)
+            send(rsend, rfar.at[core, lay - first], 8, 0, twin)
 
         @pl.when(jnp.logical_not(far))
         def _():
@@ -247,24 +262,6 @@
         pl.semaphore_wait(barrier, 3 + cols - 1)
         halo(0)
         halo(1)
-        wait_all(rbuf, len(early) - 1, recv_sem.at[0])
-        for i, l in enumerate(early):
-            for g in range(2):
-                at = g * len(early) + i
-                rall[col, at : at + 1, :] = rbuf[l, g : g + 1, :]
-        others(cols, col, lambda c: send(rall.at[col], rall.at[col], 2, 0, c))
-        wait_all(rbuf, len(late), recv_sem.at[8])
-        for i, l in enumerate(late):
-            for g in range(2):
-                at = g * len(late) + i
-                rlate[col, at : at + 1, :] = rbuf[l, g : g + 1, :]
-        others(cols, col, lambda c: send(rlate.at[col], rlate.at[col], 9, 0, c))
-        wait_all(cbuf, layers - 1, recv_sem.at[1])
-        for l in range(layers):
-            for g in range(2):
-                zmat[g * layers + l : g * layers + l + 1, :] = cbuf[l, g : g + 1, :]
-        mid = zmat.at[pl.ds(layers, layers)]
-        send(mid, zmat.at[pl.ds(2 * layers, layers)], 7, 0, right)
 
     halo_wait(0, hrecv_sem)
     for f in range(4):
@@ -285,6 +282,35 @@
     @pl.when(outer)
     def _():
         send(ksend, kbuf.at[lay], 3, 0, col)
+
+    @pl.when(center)
+    def _():
+        wait_all(rbuf, len(early) - 1, recv_sem.at[0])
+        for i, l in enumerate(early):
+            for g in range(2):
+                at = g * len(early) + i
+                rall[pair, core, at : at + 1, :] = rbuf[l, g : g + 1, :]
+        mine = rall.at[pair, core]
+        others(cols // 2, pair, lambda p: send(mine, mine, 2, 0, 2 * p + core))
+        wait_all(rfar, 2, recv_sem.at[8])
+        for i, l in enumerate(late):
+            for k in range(2):
+                for g in range(2):
+                    at = g * len(late) + i
+                    rlate[pair, k, at : at + 1, :] = rfar[k, i, g : g + 1, :]
+        both = rlate.at[pair]
+        first_ones(cols // 2, pair, 1, lambda p: send(both, both, 9, 0, 2 * p + core))
+        for i, l in enumerate(late):
+            rbuf[l] = rfar[core, i]
+        wait_all(cbuf, layers - 1, recv_sem.at[1])
+        for l in range(layers):
+            for g in range(2):
+                zmat[g * layers + l : g * layers + l + 1, :] = cbuf[l, g : g + 1, :]
+        mid = zmat.at[pl.ds(layers, layers)]
+        send(mid, zmat.at[pl.ds(2 * layers, layers)], 7, 0, right)
+        wait_all(rall.at[:, 0], cols // 2 - 1, recv_sem.at[2])
+        half = rall.at[:, core]
+        send(half, half, 10, 0, twin)
 
     @pl.when(center)
     def _():
@@ -315,11 +341,11 @@
     @pl.when(center)
     def _():
         kbuf[0] = ksend[...]
-        wait_all(rall, cols - 1, recv_sem.at[2])
+        wait_all(rall.at[:, 0], cols // 2, recv_sem.at[10])
         cut = 2 * cols * len(early)
-        total = mm(zmat[0 : 3 * layers, 0:cut], rall[...].reshape(cut, rall.shape[2]))
-        wait_all(rlate, cols - 1, recv_sem.at[9])
-        rest = rlate[...].reshape(nco - cut, rall.shape[2])
+        total = mm(zmat[0 : 3 * layers, 0:cut], rall[...].reshape(cut, rall.shape[3]))
+        wait_all(rlate, cols // 2 - 1, recv_sem.at[9])
+        rest = rlate[...].reshape(nco - cut, rlate.shape[3])
         total += mm(zmat[0 : 3 * layers, cut:nco], rest)
         for l in range(layers):
             low = (l + layers - 1) % layers
@@ -327,7 +353,8 @@
             csend[l, 1:2, :] = total[l : l + 1]
             csend[l, 2:3, :] = total[2 * layers + l : 2 * layers + l + 1]
             csend[l, 3:4, :] = total[layers + l : layers + l + 1]
-        others(layers, lay, lambda l: send(csend.at[l], crecv, 4, l, col))
+        for l in range(1, near):
+            send(csend.at[l], crecv, 4, l, col)
         wait_all(kbuf, layers - 1, recv_sem.at[3])
         base = jnp.zeros_like(a2send)
         quad = jnp.zeros_like(a2send)
@@ -347,9 +374,11 @@
         a2send[1:2, :] = base[1:2] + jnp.sum(quad, axis=0, keepdims=True)
         a2send[2:3, :] = base[2:3] + jnp.sum(cross, axis=0, keepdims=True)
         a2send[3:4, :] = base[3:4]
-        others(cols, col, lambda c: send(a2send, a2buf.at[col], 5, lay, c))
+        first_ones(cols, col, 2, lambda c: send(a2send, a2buf.at[col], 5, 0, c))
         a2buf[pl.ds(col, 1)] = a2send[...][None]
         crecv[...] = csend[0]
+        for l in range(near, layers):
+            send(csend.at[l], crecv, 4, l, col)
 
     @pl.when(outer)
     def _():
@@ -369,7 +398,8 @@
     def _():
         wait_all(a2buf, cols - 1, recv_sem.at[5])
         ssend[...] = jnp.sum(a2buf[...], axis=0)
-        others(layers, lay, lambda l: send(ssend, srecv, 6, l, col))
+        for l in range(1, layers):
+            send(ssend, srecv, 6, l, col)
         srecv[...] = ssend[...]
 
     halo_wait(2, hrecv_sem)
@@ -398,15 +428,16 @@
 
     @pl.when(center)
     def _():
-        wait_all(rall, cols - 1, send_sem.at[2])
-        wait_all(rlate, cols - 1, send_sem.at[9])
+        wait_all(rall.at[:, 0], cols // 2 - 1, send_sem.at[2])
+        wait_all(rall.at[:, 0], cols // 2, send_sem.at[10])
+        wait_all(rlate, cols // 2 - 1, send_sem.at[9])
         wait_all(csend, layers - 1, send_sem.at[4])
         wait_all(a2buf, cols - 1, send_sem.at[5])
         wait_all(csend, layers - 1, send_sem.at[6])
 
     @pl.when(outer)
     def _():
-        pl.when(far)(lambda: wait_all(rsend, 2, send_sem.at[8]))
+        pl.when(far)(lambda: wait_all(rfar.at[0], 2, send_sem.at[8]))
         pl.when(jnp.logical_not(far))(lambda: wait_all(rsend, 2, send_sem.at[0]))
         wait_all(cv, 2, send_sem.at[1])
         wait_all(ksend, 16, send_sem.at[3])
@@ -468,12 +499,13 @@
                 pltpu.VMEM((3, 4, fb, rhs), f32),
                 pltpu.VMEM((2, rhs), f32),
                 pltpu.VMEM((layers, 2, rhs), f32),
+                pltpu.VMEM((2, n_late, 2, rhs), f32),
                 pltpu.VMEM((layers, 2, nco), f32),
                 pltpu.VMEM((128, nco), f32),
                 pltpu.VMEM((nco, 128), f32),
                 pltpu.VMEM((nco, 128), f32),
-                pltpu.VMEM((cols, 2 * (layers - n_late), rhs), f32),
-                pltpu.VMEM((cols, 2 * n_late, rhs), f32),
+                pltpu.VMEM((cols // 2, 2, 2 * (layers - n_late), rhs), f32),
+                pltpu.VMEM((cols // 2, 2, 2 * n_late, rhs), f32),
                 pltpu.VMEM((16, rhs), f32),
                 pltpu.VMEM((layers, 16, rhs), f32),
                 pltpu.VMEM((layers, 4, rhs), f32),
@@ -484,8 +516,8 @@
                 pltpu.VMEM((4, rhs), f32),
                 pltpu.VMEM((4, rhs), f32),
                 pltpu.SemaphoreType.DMA((9,)),
-                pltpu.SemaphoreType.DMA((10,)),
-                pltpu.SemaphoreType.DMA((10,)),
+                pltpu.SemaphoreType.DMA((11,)),
+                pltpu.SemaphoreType.DMA((11,)),
                 pltpu.SemaphoreType.DMA((3,)),
                 pltpu.SemaphoreType.DMA((3,)),
             ],

time: 37 us -> 36.7 us (level)
  no operation moved by 1% of the time
where the time goes in v5:
time: 36.7 us; the launch traced here: 36.6 us
  Pallas kernels  35.9 us (98%)
  between operations  0.64 us (2%)
    pallas_call x1, Pallas kernels, per_device(): pl.pallas_call(functools.partial(kernel, layers, cols), out_shape=(pltpu....  35 us
    pallas_call x1, Pallas kernels, per_device(): pl.pallas_call(spread, out_shape=(field, field, field, scalar), in_specs=...  0.91 us

profile of v5, /device:TPU:1, one launch (start us, length us, event | category | flops | bytes accessed | tf_op | source)
XLA Modules:
  0.0 36.6 jit_solution(3851458408774887847)
XLA Ops:
  0.6 35.0 %shard_map.111 = (f32[3,4,128,128]{3,2,1,0:T(8,128)S(1)}, f32[1,128]{1,0:T(1,128)S(1)}) custom-call(s32[4]{0:T(128)} %bitcast.16, f32[1,128]{1,0:T(1,128)} %bitcast.17, f32[512,128]{1,0:T(8,128)} %bitcast.13, f32[4,128,128]{2,1,0:T(8,128)} %bitcast.14, f32[512,128]{1,0:T(8,128)} %bitcast.15, f32[512,512]{1,0:T(8,128)} %bitcast.11, f32[512,512]{1,0:T(8,128)} %bitcast.12, ...), custom_call_target="tpu_custom_call" | custom-call | tf_op jit(solution)/shard_map/pallas_call | solution.py:482
  35.7 0.9 %shard_map.112 = (f32[4,128,128]{2,1,0:T(8,128)}, f32[4,128,128]{2,1,0:T(8,128)}, f32[4,128,128]{2,1,0:T(8,128)}, f32[1,128]{1,0:T(1,128)}) custom-call(f32[3,4,128,128]{3,2,1,0:T(8,128)S(1)} %get-tuple-element.10.all_ref, f32[1,128]{1,0:T(1,128)S(1)} %get-tuple-element.11.rz_in), custom_call_target="tpu_custom_call" | custom-call | tf_op jit(solution)/shard_map/pallas_call | solution.py:537

commit v6 on v5

--- a/solution.py
+++ b/solution.py
@@ -394,6 +394,24 @@
     for f in range(4):
         pd[face(f), :] = pd[face(f), :] + cor[f]
 
+    for i in range(3):
+        halo_wait(i, hsend_sem)
+
+    @pl.when(center)
+    def _():
+        wait_all(rall.at[:, 0], cols // 2 - 1, send_sem.at[2])
+        wait_all(rall.at[:, 0], cols // 2, send_sem.at[10])
+        wait_all(rlate, cols // 2 - 1, send_sem.at[9])
+        wait_all(csend, layers - 1, send_sem.at[4])
+        wait_all(a2buf, cols - 1, send_sem.at[5])
+
+    @pl.when(outer)
+    def _():
+        pl.when(far)(lambda: wait_all(rfar.at[0], 2, send_sem.at[8]))
+        pl.when(jnp.logical_not(far))(lambda: wait_all(rsend, 2, send_sem.at[0]))
+        wait_all(cv, 2, send_sem.at[1])
+        wait_all(ksend, 16, send_sem.at[3])
+
     @pl.when(center)
     def _():
         wait_all(a2buf, cols - 1, recv_sem.at[5])
@@ -423,24 +441,9 @@
         image = spv[face(f), :] + beta * sqe[face(f), 0:128]
         out_ref[1, f] = rv[face(f), :] - alpha * image
 
-    for i in range(3):
-        halo_wait(i, hsend_sem)
-
-    @pl.when(center)
-    def _():
-        wait_all(rall.at[:, 0], cols // 2 - 1, send_sem.at[2])
-        wait_all(rall.at[:, 0], cols // 2, send_sem.at[10])
-        wait_all(rlate, cols // 2 - 1, send_sem.at[9])
-        wait_all(csend, layers - 1, send_sem.at[4])
-        wait_all(a2buf, cols - 1, send_sem.at[5])
+    @pl.when(center)
+    def _():
         wait_all(csend, layers - 1, send_sem.at[6])
-
-    @pl.when(outer)
-    def _():
-        pl.when(far)(lambda: wait_all(rfar.at[0], 2, send_sem.at[8]))
-        pl.when(jnp.logical_not(far))(lambda: wait_all(rsend, 2, send_sem.at[0]))
-        wait_all(cv, 2, send_sem.at[1])
-        wait_all(ksend, 16, send_sem.at[3])
 
 
 def spread(all_ref, rz_in, x_ref, r_ref, d_ref, rz_ref, sem):

time: 36.7 us -> 36.7 us (level)
  no operation moved by 1% of the time
where the time goes in v6:
time: 36.7 us; the launch traced here: 36.6 us
  Pallas kernels  35.9 us (98%)
  between operations  0.64 us (2%)
    pallas_call x1, Pallas kernels, per_device(): pl.pallas_call(functools.partial(kernel, layers, cols), out_shape=(pltpu....  35 us
    pallas_call x1, Pallas kernels, per_device(): pl.pallas_call(spread, out_shape=(field, field, field, scalar), in_specs=...  0.91 us

profile of v6, /device:TPU:1, one launch (start us, length us, event | category | flops | bytes accessed | tf_op | source)
XLA Modules:
  0.0 36.6 jit_solution(1026659198012190918)
XLA Ops:
  0.6 35.0 %shard_map.111 = (f32[3,4,128,128]{3,2,1,0:T(8,128)S(1)}, f32[1,128]{1,0:T(1,128)S(1)}) custom-call(s32[4]{0:T(128)} %bitcast.16, f32[1,128]{1,0:T(1,128)} %bitcast.17, f32[512,128]{1,0:T(8,128)} %bitcast.13, f32[4,128,128]{2,1,0:T(8,128)} %bitcast.14, f32[512,128]{1,0:T(8,128)} %bitcast.15, f32[512,512]{1,0:T(8,128)} %bitcast.11, f32[512,512]{1,0:T(8,128)} %bitcast.12, ...), custom_call_target="tpu_custom_call" | custom-call | tf_op jit(solution)/shard_map/pallas_call | solution.py:485
  35.7 0.9 %shard_map.112 = (f32[4,128,128]{2,1,0:T(8,128)}, f32[4,128,128]{2,1,0:T(8,128)}, f32[4,128,128]{2,1,0:T(8,128)}, f32[1,128]{1,0:T(1,128)}) custom-call(f32[3,4,128,128]{3,2,1,0:T(8,128)S(1)} %get-tuple-element.10.all_ref, f32[1,128]{1,0:T(1,128)S(1)} %get-tuple-element.11.rz_in), custom_call_target="tpu_custom_call" | custom-call | tf_op jit(solution)/shard_map/pallas_call | solution.py:540
